TPU v7x, 256 devices: a whole 4x4x8 slice. The times are simulated.
256 devices in a mesh: space: 64 (over y_lo, z, x), group: 4 (over y_hi, core).
Axes of the slice: x: 4, y: 4 (y_hi: 2, y_lo: 2; y = y_hi * 2 + y_lo), z: 8, core: 2. Of those that a mesh axis runs over, the one named last changes fastest.
Arguments:
- species: float32 [54, 256, 128, 128], P(None, 'space', 'group'), may hold values from 0 to 0.4
- diffusion: float32 [54], replicated, may hold values from 0.01 to 0.1
- gas_temp: float32 [256, 128, 128], P('space', 'group'), may hold values from 0.6 to 1.6
- gas_density: float32 [256, 128, 128], P('space', 'group'), may hold values from 0.5 to 2
- gas_velocity: float32 [3, 256, 128, 128], P(None, 'space', 'group'), may hold values from -1 to 1
- drop_radius: float32 [1048576], P(('space', 'group')), may hold values from 0.5 to 2
- drop_temp: float32 [1048576], P(('space', 'group')), may hold values from 0.6 to 1.2
- drop_velocity: float32 [3, 1048576], P(None, ('space', 'group')), may hold values from -2 to 2
- parcel_cells: int32 [8, 1048576], P(None, ('space', 'group')), may hold values from 0 to 98303, as said below
- parcel_weights: float32 [8, 1048576], P(None, ('space', 'group')), as said below
- parcel_counts: int32 [64], P('space'), may hold values from 2048 to 16384, as said below
Outputs:
- species_next: float32 [54, 256, 128, 128], P(None, 'space', 'group')
- gas_sources: float32 [7, 256, 128, 128], P(None, 'space', 'group')
- parcel_state: float32 [5, 1048576], P(None, ('space', 'group'))
Inputs may be any that keep to these rules, and one draw needn't show every extreme that they name: `parcel_cells`: the eight global indices of a parcel are the corners of one box of 2 x 2 x 2 cells, corner c at offsets (c // 4, c // 2 % 2, c % 2) from the first; that first cell lies in the parcel's slab or in the plane just before it, and the box lies inside the grid. `parcel_weights`: the eight weights of a parcel are non-negative trilinear weights and sum to one. `parcel_counts`: some slab is full in every draw.
All inputs are finite; a program needn't handle non-finite values.
Results may differ from a plain program's by a relative error of at most 0.000058.
Values sent between devices are 32-bit elements; how exact they have to be, the bound alone decides.
No kernel may reach another device: no remote copies, remote signals or barrier semaphores. Data moves between devices by JAX's collectives and lax.ppermute only.
A program may use at most 256 MiB of HBM per device.

v0:
```python
import jax
import jax.numpy as jnp
from jax import lax
from jax.sharding import PartitionSpec as P

time_step = 0.05
evap_coef = 0.5
heat_coef = 0.15
latent_coef = 0.2
enthalpy_coef = 1.3
source_coef = 0.5
courant = 0.3


def with_halo(block, sides, width):
    for axis, dim in sides:
        count = lax.axis_size(axis)
        forward = [(i, i + 1) for i in range(count - 1)]
        backward = [(target, source) for source, target in forward]
        low = lax.ppermute(
            lax.slice_in_dim(block, block.shape[dim] - width, None, axis=dim), axis, forward
        )
        high = lax.ppermute(lax.slice_in_dim(block, 0, width, axis=dim), axis, backward)
        block = jnp.concatenate([low, block, high], axis=dim)
    return block


def passed_along(block, axis, distance):
    devices = range(lax.axis_size(axis))
    route = [(i - distance, i) for i in devices if i - distance in devices]
    return lax.ppermute(block, axis, route)


def parcel_physics(interp, radius, drop_temp, drop_velocity):
    gas_heat = interp[0]
    density = interp[1]
    gas_speed = interp[2:5]
    fuel_vapour = interp[5]
    slip = gas_speed - drop_velocity
    slip_square = jnp.sum(slip * slip, axis=0)
    reynolds = density * radius * slip_square
    sherwood = 2.0 + 0.6 * (1.0 + reynolds) ** 0.25
    surface_fuel = 0.5 * jax.nn.sigmoid(4.0 * (drop_temp - 1.0))
    evap_rate = (
        evap_coef
        * radius
        * density
        * sherwood
        * jnp.log((1.0 - fuel_vapour) / (1.0 - surface_fuel))
    )
    drop_mass = radius * radius * radius
    mass_ratio = 1.0 - time_step * evap_rate / drop_mass
    new_radius = radius * mass_ratio ** (1.0 / 3.0)
    relax_time = 2.0 * radius * radius / (1.0 + 0.15 * (1.0 + reynolds) ** 0.35)
    new_velocity = drop_velocity + time_step / relax_time * slip
    heat_rate = heat_coef * sherwood / (radius * radius)
    new_temp = drop_temp + time_step * (
        heat_rate * (gas_heat - drop_temp) - latent_coef * evap_rate / drop_mass
    )
    vapour_mass = time_step * evap_rate
    momentum = drop_mass * (drop_velocity - new_velocity) + vapour_mass * drop_velocity
    heat_gain = -time_step * drop_mass * heat_rate * (gas_heat - drop_temp)
    enthalpy = enthalpy_coef * vapour_mass * new_temp
    drag_work = jnp.sum(drop_mass * (drop_velocity - new_velocity) * gas_speed, axis=0)
    sources = jnp.concatenate(
        [vapour_mass[None], momentum, heat_gain[None], enthalpy[None], drag_work[None]], axis=0
    )
    new_state = jnp.concatenate([new_radius[None], new_temp[None], new_velocity], axis=0)
    return (new_state, sources)


def shifted(padded, axis, offset):
    result = padded
    for which in (-3, -2, -1):
        extent = padded.shape[which]
        start_at = 2 + offset if which == axis else 2
        result = lax.slice_in_dim(result, start_at, start_at + extent - 4, axis=result.ndim + which)
    return result


def transport(padded, diffusion, speed_x, density, vapour_source, fuel_flag):
    center = shifted(padded, -1, 0)
    laplace = jnp.zeros_like(center)
    for axis in (-3, -2, -1):
        laplace = (
            laplace
            + (
                -shifted(padded, axis, 2)
                + 16.0 * shifted(padded, axis, 1)
                - 30.0 * center
                + 16.0 * shifted(padded, axis, -1)
                - shifted(padded, axis, -2)
            )
            / 12.0
        )
    gradient = (
        -shifted(padded, -3, 2)
        + 8.0 * shifted(padded, -3, 1)
        - 8.0 * shifted(padded, -3, -1)
        + shifted(padded, -3, -2)
    ) / 12.0
    return (
        center
        + diffusion * laplace
        - courant * speed_x * gradient
        + source_coef * vapour_source * (fuel_flag - center) / density
    )


def add_rims(inner, from_below, from_above):
    planes = inner.shape[1]
    inner = inner.at[:, 0:1].add(from_below)
    return inner.at[:, planes - 1 : planes].add(from_above)


def gathered_parcels(
    fields,
    parcel_cells,
    parcel_weights,
    drop_radius,
    drop_temp,
    drop_velocity,
    live,
    planes,
    rows_dev,
    depth,
    groups,
):
    slab = lax.all_gather(fields, "group", axis=2, tiled=True)
    whole = with_halo(slab, (("space", 1),), 1)
    flat_cells = parcel_cells.reshape(-1)
    flat_fields = whole.reshape(6, -1)
    corner_values = jnp.take(flat_fields, flat_cells, axis=1).reshape(6, 8, -1)
    interp = jnp.sum(corner_values * parcel_weights[None], axis=1)
    new_state, sources = parcel_physics(interp, drop_radius, drop_temp, drop_velocity)
    old_state = jnp.concatenate([drop_radius[None], drop_temp[None], drop_velocity], axis=0)
    parcel_state = jnp.where(live[None], new_state, old_state)
    sources = jnp.where(live[None], sources, jnp.zeros_like(sources))
    terms = (parcel_weights[None] * sources[:, None, :]).reshape(7, -1)
    deposit = jnp.zeros((7, flat_fields.shape[1]), jnp.float32).at[:, flat_cells].add(terms)
    deposit = deposit.reshape(7, planes + 2, rows_dev * groups, depth)
    reduced = lax.psum_scatter(deposit, "group", scatter_dimension=2, tiled=True)
    from_below = passed_along(reduced[:, planes + 1 : planes + 2], "space", 1)
    from_above = passed_along(reduced[:, 0:1], "space", -1)
    gas_sources = add_rims(reduced[:, 1 : planes + 1], from_below, from_above)
    return (gas_sources, parcel_state)


def per_device(
    species,
    diffusion,
    gas_temp,
    gas_density,
    gas_velocity,
    drop_radius,
    drop_temp,
    drop_velocity,
    parcel_cells,
    parcel_weights,
    parcel_counts,
):
    planes, rows_dev, depth = gas_temp.shape
    groups = lax.axis_size("group")
    fields = jnp.concatenate(
        [gas_temp[None], gas_density[None], gas_velocity, species[0:1]], axis=0
    )
    capacity = drop_radius.shape[0]
    slots = lax.axis_index("group") * capacity + jnp.arange(capacity, dtype=jnp.int32)
    live = slots < parcel_counts[0]
    gas_sources, parcel_state = gathered_parcels(
        fields,
        parcel_cells,
        parcel_weights,
        drop_radius,
        drop_temp,
        drop_velocity,
        live,
        planes,
        rows_dev,
        depth,
        groups,
    )
    padded = with_halo(species, (("space", 1), ("group", 2)), 2)
    padded = jnp.pad(padded, ((0, 0), (0, 0), (0, 0), (2, 2)))
    flags = (jnp.arange(species.shape[0], dtype=jnp.int32) == 0).astype(jnp.float32)
    species_next = transport(
        padded,
        diffusion[:, None, None, None],
        gas_velocity[0][None],
        gas_density[None],
        gas_sources[0][None],
        flags[:, None, None, None],
    )
    return (species_next, gas_sources, parcel_state)


def solution(mesh):
    in_specs = (
        P(None, "space", "group", None),
        P(),
        P("space", "group", None),
        P("space", "group", None),
        P(None, "space", "group", None),
        P(("space", "group")),
        P(("space", "group")),
        P(None, ("space", "group")),
        P(None, ("space", "group")),
        P(None, ("space", "group")),
        P("space"),
    )
    out_specs = (
        P(None, "space", "group", None),
        P(None, "space", "group", None),
        P(None, ("space", "group")),
    )
    return jax.shard_map(
        per_device, mesh=mesh, in_specs=in_specs, out_specs=out_specs, check_vma=False
    )
```

profile of v0, /device:TPU:1, one launch (start us, length us, event | category | flops | bytes accessed | tf_op | source)
XLA Modules:
  0.0 591.6 jit_solution(1921193020868193193)
XLA Ops:
  7.2 0.8 slice.243
  8.1 1.7 pad_maximum_fusion.12
  9.9 4.6 fusion.29
  14.5 1.3 collective-permute-start
  15.8 5.8 collective-permute-start.1
  21.9 65.4 %all-gather.2.cloned.1.call-done = f32[6,4,128,128]{3,2,1,0:T(8,128)} async-done(((f32[6,4,32,128]{3,2,1,0:T(8,128)}), f32[6,4,128,128]{3,2,1,0:T(8,128)}) %all-gather.2.cloned.1.call-update) | async-done | bytes 1572880 | tf_op jit(solution)/shard_map/all_gather | solution.py:129
  87.2 1.2 fusion.30
  88.4 1.3 collective-permute-start.4
  89.7 1.3 collective-permute-start.5
  91.8 6.4 %collective-permute-done.4 = f32[6,1,128,128]{3,2,1,0:T(8,128)S(1)} collective-permute-done((f32[6,1,128,128]{3,2,1,0:T(8,128)S(1)}, f32[6,1,128,128]{3,2,1,0:T(8,128)S(1)}, u32[]{:S(2)}, u32[]{:S(2)}) %collective-permute-start.4) | collective-permute-done | bytes 393248 | tf_op jit(solution)/shard_map/ppermute | solution.py:20
  98.2 3.9 collective-permute-done.5
  102.2 1.7 pad_maximum_fusion.8
  103.9 24.7 %copy.101 = f32[6,6,128,128]{0,3,2,1:T(8,128)} copy(f32[6,6,128,128]{3,2,1,0:T(8,128)S(1)} %pad_maximum_fusion.8) | data formatting | bytes 4718592 | tf_op jit(solution)/shard_map/concatenate | solution.py:24
  128.6 123.9 %gather_fusion = f32[32768,6]{1,0:T(8,128)} fusion(f32[6,98304]{0,1:T(8,128)} %bitcast.34, s32[32768]{0:T(1024)S(1)} %broadcast_clamp_fusion), kind=kCustom, calls=%fused_computation | custom fusion | bytes 1703936 | tf_op jit(solution)/shard_map/jit(_take)/gather | solution.py:133
  252.5 12.7 %multiply_reduce_fusion = f32[6,4096]{0,1:T(8,128)S(1)} fusion(f32[6,8,4096]{0,2,1:T(8,128)} %bitcast.35, f32[8,4096]{1,0:T(8,128)S(1)} %copy-done.7, pred[8,4096]{1,0:T(8,128)(4,1)S(1)} %compare_and_fusion), kind=kLoop, calls=%fused_computation.8 | loop fusion | flops 565248 | bytes 1048576 | tf_op jit(solution)/shard_map/reduce_sum | solution.py:134
  265.2 0.6 slice.269
  265.8 2.8 slice_reduce_fusion
  268.6 0.6 copy.109
  269.3 0.7 power_multiply_fusion
  270.0 0.6 multiply_multiply_fusion.2
  270.6 0.7 multiply_reduce_fusion.1
  271.5 0.6 copy.103
  272.1 7.6 %bitcast_multiply_fusion = f32[7,32768]{0,1:T(8,128)} fusion(f32[7,4096]{0,1:T(8,128)S(1)} %copy.103, f32[32768]{0:T(1024)S(1)} %bitcast.37), kind=kLoop, calls=%fused_computation.7 | loop fusion | flops 229376 | bytes 1163264 | tf_op jit(solution)/shard_map/mul | solution.py:139
  279.7 178.2 %scatter_custom_fusion = f32[7,98304]{0,1:T(8,128)} fusion(s32[32768]{0:T(1024)S(1)} %bitcast.40, f32[]{:T(128)} %constant.106.clone.1, f32[7,32768]{0,1:T(8,128)} %bitcast_multiply_fusion), kind=kCustom, calls=%fused_computation.2 | custom fusion | flops 229376 | bytes 3670020 | tf_op jit(solution)/shard_map/scatter-add | solution.py:140
  457.9 30.2 %copy.104 = f32[7,6,128,128]{3,2,1,0:T(8,128)} copy(f32[7,6,128,128]{0,3,2,1:T(8,128)} %bitcast.33) | data formatting | bytes 5505024 | tf_op jit(solution)/shard_map/reshape | solution.py:141
  488.2 5.3 copy.99
  493.4 3.1 copy.92
  496.5 3.9 copy.94
  500.7 3.1 collective-permute-start.2
  503.8 4.2 collective-permute-start.3
  508.0 0.8 multiply_bitcast_fusion
  508.9 0.7 copy.107
  509.5 0.7 copy.100
  510.7 0.6 broadcast_multiply_fusion.1
  511.3 0.5 collective-permute-done.2
  511.8 1.2 collective-permute-done.3
  513.0 0.8 copy-done.4
  513.8 15.6 %select_maximum_fusion = f32[54,8,36,132]{3,1,2,0:T(8,128)} fusion(f32[54,8,2,128]{3,1,2,0:T(8,128)S(1)} %collective-permute-done.2, f32[54,8,2,128]{3,1,2,0:T(8,128)S(1)} %collective-permute-done.3, f32[54,2,32,128]{3,1,2,0:T(2,128)S(1)} %copy.92, f32[54,4,32,128]{3,1,2,0:T(4,128)S(1)} %copy.99, f32[54,2,32,128]{3,1,2,0:T(2,128)S(1)} %copy.94), kind=kLoop, calls=%fused_computation.9 | loop fusion | flops 24634368 | bytes 16174080 | tf_op jit(solution)/shard_map/concatenate | solution.py:24
  529.4 2.9 reduce-scatter.2.cloned.1.call-done
  532.4 1.1 fusion.31
  533.5 3.1 collective-permute-start.6
  536.6 1.6 maximum_select_fusion
  538.2 1.3 collective-permute-start.7
  539.5 1.1 slice.272
  540.6 0.9 fusion.26
  541.5 2.2 collective-permute-done.7
  543.9 38.6 %divide_add_fusion = f32[54,4,32,128]{3,1,2,0:T(4,128)S(1)} fusion(f32[54,4,32,128]{3,1,2,0:T(4,128)S(1)} %copy.99, f32[54,8,36,132]{3,1,2,0:T(8,128)} %select_maximum_fusion, f32[54,8,2,128]{3,1,2,0:T(8,128)} %copy-done.4, f32[54,2,32,128]{3,1,2,0:T(2,128)S(1)} %copy-done.1, f32[54,2,32,128]{3,1,2,0:T(2,128)} %copy-done.2, f32[54,8,2,128]{3,1,2,0:T(8,128)} %copy-done.3, ...), kind=kLoop, calls=%fused_computation.18 | loop fusion | flops 46891008 | bytes 25854384 | tf_op jit(solution)/shard_map/add | solution.py:103
  582.5 2.2 copy.108
  (48 shorter events, 1.7 us)
Async XLA Ops:
  7.2 80.1 %all-gather.2.cloned.1.call-start = ((), (), s32[]{:S(2)}) async-start(), calls=%async_computation.1 | async-start | bytes 1966080 | tf_op jit(solution)/shard_map/all_gather | solution.py:129
  9.8 11.7 %copy-start.8 = (s32[8,4096]{1,0:T(8,128)S(1)}, s32[8,4096]{1,0:T(8,128)}, u32[]{:S(2)}) copy-start(s32[8,4096]{1,0:T(8,128)} %param.23) | copy-start | bytes 393220
  9.8 81.9 %copy-start.7 = (f32[8,4096]{1,0:T(8,128)S(1)}, f32[8,4096]{1,0:T(8,128)}, u32[]{:S(2)}) copy-start(f32[8,4096]{1,0:T(8,128)} %param.24) | copy-start | bytes 393220
  9.8 522.5 %reduce-scatter.2.cloned.1.call-start = ((), (), s32[]{:S(2)}) async-start(), calls=%async_computation.2 | async-start | bytes 3440640 | tf_op jit(solution)/shard_map/reduce_scatter | solution.py:142
  14.5 479.0 %collective-permute-start = (f32[54,2,32,128]{3,2,1,0:T(8,128)}, f32[54,2,32,128]{3,2,1,0:T(8,128)}, u32[]{:S(2)}, u32[]{:S(2)}) collective-permute-start(f32[54,2,32,128]{3,2,1,0:T(8,128)} %get-tuple-element.51), channel_id=1, source_target_pairs={{4,0},{8,4},{12,8},{16,12},{20,16},{24,20},{28,24},{32,28},{36,32}... | collective-permute-start | bytes 5308424 | tf_op jit(solution)/shard_map/ppermute | solution.py:23
  15.8 480.7 %collective-permute-start.1 = (f32[54,2,32,128]{3,2,1,0:T(8,128)}, f32[54,2,32,128]{3,2,1,0:T(8,128)}, u32[]{:S(2)}, u32[]{:S(2)}) collective-permute-start(f32[54,2,32,128]{3,2,1,0:T(8,128)} %get-tuple-element.50), channel_id=1, source_target_pairs={{0,4},{4,8},{8,12},{12,16},{16,20},{20,24},{24,28},{28,32},{32,36}... | collective-permute-start | bytes 5308424 | tf_op jit(solution)/shard_map/ppermute | solution.py:20
  88.4 9.8 %collective-permute-start.4 = (f32[6,1,128,128]{3,2,1,0:T(8,128)S(1)}, f32[6,1,128,128]{3,2,1,0:T(8,128)S(1)}, u32[]{:S(2)}, u32[]{:S(2)}) collective-permute-start(f32[6,1,128,128]{3,2,1,0:T(8,128)S(1)} %get-tuple-element.52), channel_id=1, source_target_pairs={{0,4},{4,8},{8,12},{12,16},{16,20},{20,24},{24,28},{28,32},{32,36}... | collective-permute-start | bytes 1179656 | tf_op jit(solution)/shard_map/ppermute | solution.py:20
  89.7 12.4 %collective-permute-start.5 = (f32[6,1,128,128]{3,2,1,0:T(8,128)S(1)}, f32[6,1,128,128]{3,2,1,0:T(8,128)}, u32[]{:S(2)}, u32[]{:S(2)}) collective-permute-start(f32[6,1,128,128]{3,2,1,0:T(8,128)S(1)} %get-tuple-element.53), channel_id=1, source_target_pairs={{4,0},{8,4},{12,8},{16,12},{20,16},{24,20},{28,24},{32,28},{36,32}... | collective-permute-start | bytes 1179656 | tf_op jit(solution)/shard_map/ppermute | solution.py:23
  91.8 179.6 %copy-start.12 = (pred[4096]{0:T(1024)(128)(4,1)}, pred[4096]{0:T(1024)(128)(4,1)S(1)}, u32[]{:S(2)}) copy-start(pred[4096]{0:T(1024)(128)(4,1)S(1)} %add_compare_fusion) | copy-start | bytes 12292
  265.8 3.5 copy-start.6
  265.8 3.5 copy-start.10
  265.8 3.5 copy-start.11
  496.5 16.5 %copy-start = (f32[54,2,32,128]{3,1,2,0:T(2,128)}, f32[54,2,32,128]{3,1,2,0:T(2,128)S(1)}, u32[]{:S(2)}) copy-start(f32[54,2,32,128]{3,1,2,0:T(2,128)S(1)} %copy.92) | copy-start | bytes 5308420
  500.4 12.6 %copy-start.2 = (f32[54,2,32,128]{3,1,2,0:T(2,128)}, f32[54,2,32,128]{3,1,2,0:T(2,128)S(1)}, u32[]{:S(2)}) copy-start(f32[54,2,32,128]{3,1,2,0:T(2,128)S(1)} %copy.94) | copy-start | bytes 5308420
  500.4 8.5 %copy-start.9 = (f32[4,32,128]{2,1,0:T(8,128)S(1)}, f32[4,32,128]{2,1,0:T(8,128)}, u32[]{:S(2)}) copy-start(f32[4,32,128]{2,1,0:T(8,128)} %param.18) | copy-start | bytes 196612
  500.4 10.3 %copy-start.13 = (f32[54]{0:T(128)S(1)}, f32[54]{0:T(128)}, u32[]{:S(2)}) copy-start(f32[54]{0:T(128)} %param.16) | copy-start | bytes 652
  500.7 11.1 %collective-permute-start.2 = (f32[54,8,2,128]{3,1,2,0:T(8,128)S(1)}, f32[54,8,2,128]{3,1,2,0:T(8,128)S(1)}, u32[]{:S(2)}, u32[]{:S(2)}) collective-permute-start(f32[54,8,2,128]{3,1,2,0:T(8,128)S(1)} %get-tuple-element.49), channel_id=1, source_target_pairs={{1,0},{2,1},{3,2},{5,4},{6,5},{7,6},{9,8},{10,9},{11,10},{13,12},{... | collective-permute-start | bytes 1327112 | tf_op jit(solution)/shard_map/ppermute | solution.py:23
  503.8 9.2 %collective-permute-start.3 = (f32[54,8,2,128]{3,1,2,0:T(8,128)S(1)}, f32[54,8,2,128]{3,1,2,0:T(8,128)S(1)}, u32[]{:S(2)}, u32[]{:S(2)}) collective-permute-start(f32[54,8,2,128]{3,1,2,0:T(8,128)S(1)} %get-tuple-element.48), channel_id=1, source_target_pairs={{0,1},{1,2},{2,3},{4,5},{5,6},{6,7},{8,9},{9,10},{10,11},{12,13},{... | collective-permute-start | bytes 1327112 | tf_op jit(solution)/shard_map/ppermute | solution.py:20
  511.8 1.2 copy-start.3
  513.0 0.8 copy-start.4
  532.4 11.5 %copy-start.1 = (f32[54,2,32,128]{3,1,2,0:T(2,128)S(1)}, f32[54,2,32,128]{3,1,2,0:T(2,128)}, u32[]{:S(2)}) copy-start(f32[54,2,32,128]{3,1,2,0:T(2,128)} %copy-done) | copy-start | bytes 5308420
  533.5 7.1 %collective-permute-start.6 = (f32[7,1,32,128]{3,2,1,0:T(8,128)S(1)}, f32[7,1,32,128]{3,2,1,0:T(8,128)S(1)}, u32[]{:S(2)}, u32[]{:S(2)}) collective-permute-start(f32[7,1,32,128]{3,2,1,0:T(8,128)S(1)} %get-tuple-element.55), channel_id=1, source_target_pairs={{0,4},{4,8},{8,12},{12,16},{16,20},{20,24},{24,28},{28,32},{32,36}... | collective-permute-start | bytes 344072 | tf_op jit(solution)/shard_map/ppermute | solution.py:31
  538.2 5.5 collective-permute-start.7
  543.8 38.7 %copy-start.5 = (f32[7,4,32,128]{3,2,1,0:T(8,128)}, f32[7,4,32,128]{3,2,1,0:T(8,128)S(1)}, u32[]{:S(2)}) copy-start(f32[7,4,32,128]{3,2,1,0:T(8,128)S(1)} %fusion.25) | copy-start | bytes 1376260
Sparse Core Ops, SparseCore 0:
  10.4 76.8 all-gather.1
  488.3 44.0 reduce-scatter.1
where the time goes:
time: 597 us; the launch traced here: 592 us
  other arithmetic  266 us (45%)
  local copies, waits for them, and re-layouts  206 us (35%)
  waiting for transfers between devices  82.7 us (14%)
  starting transfers between devices  21.4 us (4%)
  between operations  15.1 us (3%)
    scatter-add x1, other arithmetic, gathered_parcels(): jnp.zeros((7, flat_fields.shape[1]), jnp.float32).at[:, flat_cells]  178 us
    gather x1, local copies, waits for them, and re-layouts, gathered_parcels(): corner_values = jnp.take(flat_fields, flat_cells, axis=1).reshape(6, 8, -1)  124 us
    all_gather x1, waiting for transfers between devices, gathered_parcels(): slab = lax.all_gather(fields, 'group', axis=2, tiled=True)  65.4 us
    add x1, other arithmetic, transport(): center + diffusion * laplace - courant * speed_x * gradient  38.6 us
    reshape x1, local copies, waits for them, and re-layouts, gathered_parcels(): deposit = deposit.reshape(7, planes + 2, rows_dev * groups, depth)  30.2 us
    concatenate x1, local copies, waits for them, and re-layouts, with_halo(): block = jnp.concatenate([low, block, high], axis=dim)  24.7 us
    concatenate x3, other arithmetic, with_halo(): block = jnp.concatenate([low, block, high], axis=dim)  17.6 us
    reduce_sum x1, other arithmetic, gathered_parcels(): interp = jnp.sum(corner_values * parcel_weights[None], axis=1)  12.7 us
  transfers between devices with their start and end apart: 10, of which 7 were waited for; matrix products, arithmetic and copies ran while one was open for 72% of the time, Pallas kernels for 0%

commit v1 on v0

v1 whole, which is shorter than its diff:
```python
import jax
import jax.numpy as jnp
from jax import lax
from jax.experimental import pallas as pl
from jax.experimental.pallas import tpu as pltpu
from jax.sharding import PartitionSpec as P

time_step = 0.05
evap_coef = 0.5
heat_coef = 0.15
latent_coef = 0.2
enthalpy_coef = 1.3
source_coef = 0.5
courant = 0.3

LANES = 128
CHUNK = 512
PHYS = 1024
WINDOW = 256
YPAD = 40
F32 = jnp.float32
BF16 = jnp.bfloat16
NT = (((1,), (1,)), ((), ()))


def halves(value):
    high = value.astype(BF16)
    return high, (value - high.astype(F32)).astype(BF16)


def hat(index, start, fraction):
    away = index - start
    return jnp.where(away == 0.0, 1.0 - fraction, jnp.where(away == 1.0, fraction, 0.0))


def iota(shape, dim):
    return lax.broadcasted_iota(jnp.int32, shape, dim)


def one_hot(dst_row, aligned):
    rel = dst_row - aligned.astype(F32)
    return jnp.where(iota((WINDOW, LANES), 0).astype(F32) == rel, 1.0, 0.0).astype(BF16)


def physics(interp, radius, drop_temp, velocity):
    heat, density, speed, fuel = interp[0], interp[1], interp[2:5], interp[5]
    slip = [g - v for g, v in zip(speed, velocity)]
    slip_square = slip[0] * slip[0] + slip[1] * slip[1] + slip[2] * slip[2]
    log_flow = jnp.log(1.0 + density * radius * slip_square)
    sherwood = 2.0 + 0.6 * jnp.exp(0.25 * log_flow)
    surface = 0.5 / (1.0 + jnp.exp(-4.0 * (drop_temp - 1.0)))
    evap = evap_coef * radius * density * sherwood * jnp.log((1.0 - fuel) / (1.0 - surface))
    mass = radius * radius * radius
    ratio = 1.0 - time_step * evap / mass
    new_radius = radius * jnp.exp(jnp.log(ratio) * (1.0 / 3.0))
    rate = time_step * (1.0 + 0.15 * jnp.exp(0.35 * log_flow)) / (2.0 * radius * radius)
    change = [rate * s for s in slip]
    new_velocity = [v + c for v, c in zip(velocity, change)]
    heat_rate = heat_coef * sherwood / (radius * radius)
    new_temp = drop_temp + time_step * (
        heat_rate * (heat - drop_temp) - latent_coef * evap / mass
    )
    vapour = time_step * evap
    lost = [mass * (v - n) for v, n in zip(velocity, new_velocity)]
    momentum = [m + vapour * v for m, v in zip(lost, velocity)]
    heat_gain = -time_step * mass * heat_rate * (heat - drop_temp)
    enthalpy = enthalpy_coef * vapour * new_temp
    drag = lost[0] * speed[0] + lost[1] * speed[1] + lost[2] * speed[2]
    return [new_radius, new_temp] + new_velocity, [vapour] + momentum + [heat_gain, enthalpy, drag]


def parcel_kernel(
    info_ref,
    pk_ref,
    lo_ref,
    temp_ref,
    dens_ref,
    vel_ref,
    fuel_ref,
    hi_ref,
    yrow_ref,
    main_ref,
    dlo_ref,
    dhi_ref,
    dy_ref,
    state_ref,
    dst_ref,
    off_ref,
    cell_scr,
    off_smem,
    sem,
    pieces,
    cv,
    row_scr,
    ft,
    a_hi,
    a_lo,
    interp,
    src,
    dep,
):
    slots = pk_ref.shape[1]
    blocks = slots // LANES
    count, group = info_ref[0], info_ref[1]

    for b in range(blocks):
        cell_scr[b : b + 1, :] = pk_ref[8:9, b * LANES : (b + 1) * LANES]
    cell = cell_scr[...].astype(jnp.int32)
    slot = iota((blocks, LANES), 0) * LANES + iota((blocks, LANES), 1)
    mine = jnp.logical_and(slot < count, ((cell >> 12) & 3) == group)
    ones = jnp.where(mine, 1.0, 0.0).astype(BF16)
    before = jnp.where(iota((LANES, LANES), 0) < iota((LANES, LANES), 1), 1.0, 0.0).astype(BF16)
    after = jnp.where(iota((LANES, LANES), 1) < iota((LANES, LANES), 0), 1.0, 0.0).astype(BF16)
    full = jnp.ones((LANES, LANES), BF16)
    within = jnp.dot(ones, before, preferred_element_type=F32)
    row_sum = jnp.dot(ones, full, preferred_element_type=F32).astype(BF16)
    offset = jnp.dot(after, row_sum, preferred_element_type=F32)
    dst_ref[...] = jnp.where(mine, within + offset, -1.0)
    counts = lax.dot_general(jnp.ones((16, LANES), BF16), ones, NT, preferred_element_type=F32)
    counts = counts.astype(BF16)
    starts = jnp.dot(counts, before, preferred_element_type=F32)
    total = jnp.dot(counts, full, preferred_element_type=F32)
    first = iota((8, LANES), 0) == 0
    off_ref[...] = jnp.where(first, starts[0:8], total[0:8]).astype(jnp.int32)
    copy = pltpu.make_async_copy(off_ref, off_smem, sem)
    copy.start()

    def split(c, carry):
        at = pl.ds(pl.multiple_of(c * 2048, 2048), 2048)
        cells = jnp.broadcast_to(pk_ref[8:9, at], (8, 2048)).astype(jnp.int32)
        row = iota((8, 2048), 0)
        place = jnp.where(
            row == 0, cells >> 14, jnp.where(row == 1, (cells >> 7) & 31, cells & 127)
        ).astype(F32)
        high, low = halves(jnp.concatenate([pk_ref[0:8, at], place], axis=0))
        pieces[0:16, at] = high
        pieces[16:32, at] = low
        return carry

    lax.fori_loop(0, slots // 2048, split, 0)

    zero = jnp.zeros((256, LANES), F32)
    own = [temp_ref, dens_ref, vel_ref.at[0], vel_ref.at[1], vel_ref.at[2], fuel_ref.at[0]]
    planes = temp_ref.shape[0]
    rows = temp_ref.shape[1]
    for f in range(6):
        row_scr[...] = zero
        for x in range(planes + 2):
            if x == 0:
                block = lo_ref[f, 0]
            elif x == planes + 1:
                block = hi_ref[f, 0]
            else:
                block = own[f][x - 1]
            row_scr[x * YPAD : x * YPAD + rows, :] = block
            row_scr[x * YPAD + rows : x * YPAD + rows + 1, :] = yrow_ref[f, x]
        high, low = halves(row_scr[...].T)
        at = slice(f * LANES, (f + 1) * LANES)
        ft[at, 0:256] = high
        ft[at, 256:512] = low
        ft[at, 512:768] = high

    cv[...] = jnp.zeros(cv.shape, F32)
    state_ref[...] = jnp.zeros(state_ref.shape, F32)
    dep[...] = jnp.zeros(dep.shape, F32)
    copy.wait()
    live = off_smem[1, 0]

    def compact(i, carry):
        got = []
        for j in range(8):
            b = i * 8 + j
            aligned = (off_smem[0, b] >> 7) << 7
            hot = one_hot(dst_ref[pl.ds(b, 1), :], aligned)
            block = pieces[:, pl.ds(pl.multiple_of(b * LANES, LANES), LANES)]
            got.append((aligned, lax.dot_general(block, hot, NT, preferred_element_type=F32)))
        for aligned, both in got:
            at = pl.ds(pl.multiple_of(aligned, LANES), WINDOW)
            cv[:, at] += both[0:16] + both[16:32]
        return carry

    lax.fori_loop(0, blocks // 8, compact, 0)

    def gather(c, carry):
        at = pl.ds(pl.multiple_of(c * CHUNK, CHUNK), CHUNK)
        valid = c * CHUNK + iota((1, CHUNK), 1) < live
        fx, fy, fz = cv[0:1, at], cv[1:2, at], cv[2:3, at]
        x0, z0 = cv[8:9, at], cv[10:11, at]
        y0 = jnp.where(valid, cv[9:10, at], 1000.0)
        wy = hat(iota((YPAD, CHUNK), 0).astype(F32), y0, fy)
        parts = [wy * hat(float(x), x0, fx) for x in range(planes + 2)]
        parts.append(jnp.zeros((256 - (planes + 2) * YPAD, CHUNK), F32))
        high, low = halves(jnp.concatenate(parts, axis=0))
        a_hi[c] = high
        a_lo[c] = low
        stacked = jnp.concatenate([high, high, low], axis=0)
        lines = jnp.dot(ft[...], stacked, preferred_element_type=F32)
        wz = hat(iota((LANES, CHUNK), 0).astype(F32), z0, fz)
        for f in range(6):
            interp[f : f + 1, at] = jnp.sum(
                lines[f * LANES : (f + 1) * LANES] * wz, axis=0, keepdims=True
            )
        return carry

    chunks = (live + CHUNK - 1) // CHUNK
    lax.fori_loop(0, chunks, gather, 0)

    def step(c, carry):
        at = pl.ds(pl.multiple_of(c * PHYS, PHYS), PHYS)
        valid = c * PHYS + iota((1, PHYS), 1) < live
        inside = [jnp.where(valid, interp[f : f + 1, at], 0.0) for f in range(6)]
        radius = jnp.where(valid, cv[3:4, at], 1.0)
        velocity = [cv[d : d + 1, at] for d in (5, 6, 7)]
        new, sources = physics(inside, radius, cv[4:5, at], velocity)
        for s in range(5):
            state_ref[s : s + 1, at] = jnp.where(valid, new[s], 0.0)
        for k in range(7):
            src[k : k + 1, at] = jnp.where(valid, sources[k], 0.0)
        return carry

    lax.fori_loop(0, (live + PHYS - 1) // PHYS, step, 0)

    def deposit(c, carry):
        at = pl.ds(pl.multiple_of(c * CHUNK, CHUNK), CHUNK)
        wz = hat(iota((LANES, CHUNK), 0).astype(F32), cv[10:11, at], cv[2:3, at])
        high, low = halves(jnp.concatenate([wz * src[k : k + 1, at] for k in range(7)], axis=0))
        left = jnp.concatenate([high, low, high], axis=1)
        right = jnp.concatenate([a_hi[c], a_hi[c], a_lo[c]], axis=1)
        dep[...] += lax.dot_general(left, right, NT, preferred_element_type=F32)
        return carry

    lax.fori_loop(0, chunks, deposit, 0)

    for k in range(7):
        cells = dep[k * LANES : (k + 1) * LANES, :].T
        for x in range(planes + 2):
            block = cells[x * YPAD : x * YPAD + rows]
            if x == 0:
                dlo_ref[k, 0] = block
            elif x == planes + 1:
                dhi_ref[k, 0] = block
            else:
                main_ref[k, x - 1] = block
            dy_ref[k, x] = cells[x * YPAD + rows : x * YPAD + rows + 1]


def spread_kernel(off_ref, dst_ref, state_ref, out_ref, both_scr):
    high, low = halves(state_ref[...])
    both_scr[0:16, :] = jnp.concatenate([high, low], axis=0)

    def spread(i, carry):
        for j in range(8):
            b = i * 8 + j
            aligned = (off_ref[0, b] >> 7) << 7
            hot = one_hot(dst_ref[pl.ds(b, 1), :], aligned)
            block = both_scr[:, pl.ds(pl.multiple_of(aligned, LANES), WINDOW)]
            got = jnp.dot(block, hot, preferred_element_type=F32)
            out_ref[:, pl.ds(pl.multiple_of(b * LANES, LANES), LANES)] = got[0:8] + got[8:16]
        return carry

    lax.fori_loop(0, dst_ref.shape[0] // 8, spread, 0)


def species_kernel(
    diff_ref, y_ref, xlo_ref, xhi_ref, ylo_ref, yhi_ref, ux_ref, dens_ref, vap_ref, out_ref, pad
):
    species, planes, rows, depth = y_ref.shape
    at = iota((rows, depth), 1)
    left1 = jnp.where(at >= 1, 16.0, 0.0)
    left2 = jnp.where(at >= 2, -1.0, 0.0)
    right1 = jnp.where(at < depth - 1, 16.0, 0.0)
    right2 = jnp.where(at < depth - 2, -1.0, 0.0)
    first = pl.program_id(0) * species
    for x in range(planes):
        speed = ux_ref[x] * (courant / 12.0)
        gain = source_coef * vap_ref[x] / dens_ref[x]

        def one(s, carry):
            d12 = diff_ref[first + s] * (1.0 / 12.0)

            def plane(i):
                if i < 0:
                    return xlo_ref[s, i + 2]
                if i >= planes:
                    return xhi_ref[s, i - planes]
                return y_ref[s, i]

            center = plane(x)
            up1, up2, dn1, dn2 = plane(x + 1), plane(x + 2), plane(x - 1), plane(x - 2)
            pad[6:8, :] = ylo_ref[s, x]
            pad[8 : 8 + rows, :] = center
            pad[8 + rows : 10 + rows, :] = yhi_ref[s, x]
            near = up1 + dn1 + pad[7 : 7 + rows, :] + pad[9 : 9 + rows, :]
            far = up2 + dn2 + pad[6 : 6 + rows, :] + pad[10 : 10 + rows, :]
            along = (
                left1 * pltpu.roll(center, 1, 1)
                + right1 * pltpu.roll(center, depth - 1, 1)
                + left2 * pltpu.roll(center, 2, 1)
                + right2 * pltpu.roll(center, depth - 2, 1)
            )
            slope = 8.0 * (up1 - dn1) - (up2 - dn2)
            flag = jnp.where(first + s == 0, 1.0, 0.0)
            laplace = 16.0 * near - far + along - 90.0 * center
            out_ref[s, x] = center + d12 * laplace - speed * slope + gain * (flag - center)
            return carry

        lax.fori_loop(0, species, one, 0, unroll=True)


def per_device(
    species,
    diffusion,
    gas_temp,
    gas_density,
    gas_velocity,
    drop_radius,
    drop_temp,
    drop_velocity,
    parcel_cells,
    parcel_weights,
    parcel_counts,
):
    count_s = lax.axis_size("space")
    groups = lax.axis_size("group")
    planes, rows, depth = gas_temp.shape
    kinds = species.shape[0]
    capacity = drop_radius.shape[0]
    slots = capacity * groups
    blocks = slots // LANES
    ahead = [(i, i + 1) for i in range(count_s - 1)]
    back = [(b, a) for a, b in ahead]
    g_ahead = [(i, i + 1) for i in range(groups - 1)]
    g_back = [(b, a) for a, b in g_ahead]
    group = lax.axis_index("group")

    def upper(chosen):
        return sum(parcel_weights[c : c + 1] for c in chosen)

    packed = jnp.concatenate(
        [
            upper((4, 5, 6, 7)),
            upper((2, 3, 6, 7)),
            upper((1, 3, 5, 7)),
            drop_radius[None],
            drop_temp[None],
            drop_velocity,
            parcel_cells[0:1].astype(F32),
        ],
        axis=0,
    )
    parcels = lax.all_gather(packed, "group", axis=1, tiled=True)

    def rim(x):
        return jnp.concatenate(
            [gas_temp[None, x : x + 1], gas_density[None, x : x + 1], gas_velocity[:, x : x + 1],
             species[0:1, x : x + 1]],
            axis=0,
        )

    field_lo = lax.ppermute(rim(planes - 1), "space", ahead)
    field_hi = lax.ppermute(rim(0), "space", back)
    own_row = jnp.concatenate(
        [gas_temp[None, :, 0:1], gas_density[None, :, 0:1], gas_velocity[:, :, 0:1],
         species[0:1, :, 0:1]],
        axis=0,
    )
    row = jnp.concatenate([field_lo[:, :, 0:1], own_row, field_hi[:, :, 0:1]], axis=1)
    row = lax.ppermute(row, "group", g_back)

    x_lo = lax.ppermute(species[:, planes - 2 :], "space", ahead)
    x_hi = lax.ppermute(species[:, 0:2], "space", back)
    y_lo = lax.ppermute(species[:, :, rows - 2 :], "group", g_ahead)
    y_hi = lax.ppermute(species[:, :, 0:2], "group", g_back)

    info = jnp.stack([parcel_counts[0], group.astype(jnp.int32)])
    whole = lambda shape: pl.BlockSpec(shape, lambda i, n=len(shape): (0,) * n)
    smem = pl.BlockSpec(memory_space=pltpu.SMEM)
    reach = slots + WINDOW
    main, dep_lo, dep_hi, dep_y, state, dst, off = pl.pallas_call(
        parcel_kernel,
        grid=(1,),
        in_specs=[
            smem,
            whole((9, slots)),
            whole((6, 1, rows, depth)),
            whole((planes, rows, depth)),
            whole((planes, rows, depth)),
            whole((3, planes, rows, depth)),
            whole((1, planes, rows, depth)),
            whole((6, 1, rows, depth)),
            whole((6, planes + 2, 1, depth)),
        ],
        out_specs=[
            whole((7, planes, rows, depth)),
            whole((7, 1, rows, depth)),
            whole((7, 1, rows, depth)),
            whole((7, planes + 2, 1, depth)),
            whole((8, reach)),
            whole((blocks, LANES)),
            whole((8, LANES)),
        ],
        out_shape=[
            jax.ShapeDtypeStruct((7, planes, rows, depth), F32),
            jax.ShapeDtypeStruct((7, 1, rows, depth), F32),
            jax.ShapeDtypeStruct((7, 1, rows, depth), F32),
            jax.ShapeDtypeStruct((7, planes + 2, 1, depth), F32),
            jax.ShapeDtypeStruct((8, reach), F32),
            jax.ShapeDtypeStruct((blocks, LANES), F32),
            jax.ShapeDtypeStruct((8, LANES), jnp.int32),
        ],
        scratch_shapes=[
            pltpu.VMEM((blocks, LANES), F32),
            pltpu.SMEM((8, LANES), jnp.int32),
            pltpu.SemaphoreType.DMA,
            pltpu.VMEM((32, slots), BF16),
            pltpu.VMEM((16, reach), F32),
            pltpu.VMEM((256, LANES), F32),
            pltpu.VMEM((6 * LANES, 768), BF16),
            pltpu.VMEM((slots // CHUNK, 256, CHUNK), BF16),
            pltpu.VMEM((slots // CHUNK, 256, CHUNK), BF16),
            pltpu.VMEM((8, slots), F32),
            pltpu.VMEM((8, slots), F32),
            pltpu.VMEM((7 * LANES, 256), F32),
        ],
        compiler_params=pltpu.CompilerParams(vmem_limit_bytes=50 * 2**20),
        name="parcels",
    )(info, parcels, field_lo, gas_temp, gas_density, gas_velocity, species, field_hi, row)

    from_y = lax.ppermute(dep_y, "group", g_ahead)
    dep_lo = dep_lo.at[:, :, 0:1].add(from_y[:, 0:1])
    dep_hi = dep_hi.at[:, :, 0:1].add(from_y[:, planes + 1 :])
    from_below = lax.ppermute(dep_hi, "space", ahead)
    from_above = lax.ppermute(dep_lo, "space", back)
    gas_sources = main.at[:, :, 0:1].add(from_y[:, 1 : planes + 1])
    gas_sources = gas_sources.at[:, 0:1].add(from_below)
    gas_sources = gas_sources.at[:, planes - 1 :].add(from_above)

    spread = pl.pallas_call(
        spread_kernel,
        grid=(1,),
        in_specs=[smem, whole((blocks, LANES)), whole((8, reach))],
        out_specs=whole((8, slots)),
        out_shape=jax.ShapeDtypeStruct((8, slots), F32),
        scratch_shapes=[pltpu.VMEM((16, reach), BF16)],
        compiler_params=pltpu.CompilerParams(vmem_limit_bytes=24 * 2**20),
        name="spread",
    )(off, dst, state)

    def part(owner):
        return lax.dynamic_slice_in_dim(spread, owner * capacity, capacity, axis=1)

    new_state = part(group)
    for d in range(1, groups):
        route = [(i, (i + d) % groups) for i in range(groups)]
        new_state = new_state + lax.ppermute(part((group + d) % groups), "group", route)
    old_state = jnp.concatenate([drop_radius[None], drop_temp[None], drop_velocity], axis=0)
    slot = group * capacity + jnp.arange(capacity, dtype=jnp.int32)
    live = slot < parcel_counts[0]
    parcel_state = jnp.where(live[None], new_state[0:5], old_state)

    many = 6
    by_kind = lambda *shape: pl.BlockSpec((many,) + shape, lambda i: (i, 0, 0, 0))
    gas = pl.BlockSpec((planes, rows, depth), lambda i: (0, 0, 0))
    species_next = pl.pallas_call(
        species_kernel,
        grid=(kinds // many,),
        in_specs=[
            smem,
            by_kind(planes, rows, depth),
            by_kind(2, rows, depth),
            by_kind(2, rows, depth),
            by_kind(planes, 2, depth),
            by_kind(planes, 2, depth),
            pl.BlockSpec((None, planes, rows, depth), lambda i: (0, 0, 0, 0)),
            gas,
            pl.BlockSpec((None, planes, rows, depth), lambda i: (0, 0, 0, 0)),
        ],
        out_specs=by_kind(planes, rows, depth),
        out_shape=jax.ShapeDtypeStruct(species.shape, F32),
        scratch_shapes=[pltpu.VMEM((rows + 16, depth), F32)],
        compiler_params=pltpu.CompilerParams(vmem_limit_bytes=24 * 2**20),
        name="transport",
    )(diffusion, species, x_lo, x_hi, y_lo, y_hi, gas_velocity, gas_density, gas_sources)
    return (species_next, gas_sources, parcel_state)


def solution(mesh):
    in_specs = (
        P(None, "space", "group", None),
        P(),
        P("space", "group", None),
        P("space", "group", None),
        P(None, "space", "group", None),
        P(("space", "group")),
        P(("space", "group")),
        P(None, ("space", "group")),
        P(None, ("space", "group")),
        P(None, ("space", "group")),
        P("space"),
    )
    out_specs = (
        P(None, "space", "group", None),
        P(None, "space", "group", None),
        P(None, ("space", "group")),
    )
    return jax.shard_map(
        per_device, mesh=mesh, in_specs=in_specs, out_specs=out_specs, check_vma=False
    )
```

time: 597 us -> 163 us (0.27)
  other arithmetic: 266 us -> 8.42 us
  local copies, waits for them, and re-layouts: 206 us -> 28 us
  waiting for transfers between devices: 82.7 us -> 8.1 us
  blocking collectives: 0 us -> 51.5 us
  Pallas kernels: 0 us -> 34.3 us
  between operations: 15.1 us -> 1.62 us
  starting transfers between devices: 21.4 us -> 29.9 us
    scatter-add x3 -> x2, other arithmetic: 179 us -> 3.13 us  [the longest x1 1.57 us: per_device(): gas_sources = gas_sources.at[:, 0:1].add(from_below)]
    gather x1 -> x0, local copies, waits for them, and re-layouts: 124 us -> none  [gathered_parcels(): corner_values = jnp.take(flat_fields, flat_cells, axis=1).reshape(6, 8, -1)]
    all_gather x1 -> x0, waiting for transfers between devices: 65.4 us -> none  [gathered_parcels(): slab = lax.all_gather(fields, 'group', axis=2, tiled=True)]
    all_gather x0 -> x1, blocking collectives: none -> 51.5 us  [per_device(): parcels = lax.all_gather(packed, 'group', axis=1, tiled=True)]
    add x1 -> x3, other arithmetic: 38.6 us -> 2.4 us  [the longest x1 1.51 us: per_device(): gas_sources = main.at[:, :, 0:1].add(from_y[:, 1:planes + 1])]
    pallas_call x0 -> x3, Pallas kernels: none -> 34.3 us  [the longest x1 21 us: per_device(): pl.pallas_call(parcel_kernel, grid=(1,), in_specs=[smem, whole((9, slots)...]
    reshape x1 -> x0, local copies, waits for them, and re-layouts: 30.2 us -> none  [gathered_parcels(): deposit = deposit.reshape(7, planes + 2, rows_dev * groups, depth)]
    concatenate x2 -> x1, local copies, waits for them, and re-layouts: 24.8 us -> 0.18 us  [per_device(): jnp.concatenate([upper((4, 5, 6, 7)), upper((2, 3, 6, 7)), upper((1, 3, 5...]
  transfers between devices with their start and end apart: 10 -> 13, of which waited for: 7 -> 3; matrix products, arithmetic and copies ran while one was open for 72% -> 14% of each run, Pallas kernels for 0% -> 15%
where the time goes in v1:
time: 163 us; the launch traced here: 162 us
  blocking collectives  51.5 us (32%)
  Pallas kernels  34.3 us (21%)
  starting transfers between devices  29.9 us (18%)
  local copies, waits for them, and re-layouts  28 us (17%)
  other arithmetic  8.42 us (5%)
  waiting for transfers between devices  8.1 us (5%)
    all_gather x1, blocking collectives, per_device(): parcels = lax.all_gather(packed, 'group', axis=1, tiled=True)  51.5 us
    pallas_call x1, Pallas kernels, per_device(): pl.pallas_call(parcel_kernel, grid=(1,), in_specs=[smem, whole((9, slots)...  21 us
    unnamed x46, local copies, waits for them, and re-layouts  11.2 us
    pallas_call x1, Pallas kernels, per_device(): pl.pallas_call(species_kernel, grid=(kinds // many,), in_specs=[smem, by_...  9.41 us
    ppermute x1, starting transfers between devices, per_device(): x_lo = lax.ppermute(species[:, planes - 2:], 'space', ahead)  5.82 us
    slice x1, local copies, waits for them, and re-layouts, per_device(): x_hi = lax.ppermute(species[:, 0:2], 'space', back)  4.52 us
    ppermute x1, starting transfers between devices, per_device(): y_lo = lax.ppermute(species[:, :, rows - 2:], 'group', g_ahead)  4.47 us
    ppermute x1, waiting for transfers between devices, per_device(): row = lax.ppermute(row, 'group', g_back)  4.44 us
  transfers between devices with their start and end apart: 13, of which 3 were waited for; matrix products, arithmetic and copies ran while one was open for 14% of the time, Pallas kernels for 15%

profile of v1, /device:TPU:1, one launch (start us, length us, event | category | flops | bytes accessed | tf_op | source)
XLA Modules:
  0.0 161.8 jit_solution(10807853790249842229)
XLA Ops:
  0.6 0.7 fusion.3
  1.4 0.8 fusion.6
  2.2 0.8 slice_bitcast_fusion
  3.0 4.0 %collective-permute-start.4 = (f32[6,1,32,128]{3,2,1,0:T(8,128)S(1)}, f32[6,1,32,128]{3,2,1,0:T(8,128)S(1)}, u32[]{:S(2)}, u32[]{:S(2)}) collective-permute-start(f32[6,1,32,128]{3,2,1,0:T(8,128)S(1)} %pad_maximum_fusion), channel_id=1, source_target_pairs={{0,4},{4,8},{8,12},{12,16},{16,20},{20,24},{24,28},{28,32},{32,36}... | collective-permute-start | bytes 294920 | tf_op jit(solution)/shard_map/ppermute | solution.py:360
  7.0 1.4 collective-permute-start.5
  8.4 4.5 %fusion.5 = (f32[54,2,32,128]{3,2,1,0:T(8,128)}, f32[54,2,32,128]{3,2,1,0:T(8,128)}) fusion(f32[54,4,32,128]{3,2,1,0:T(8,128)} %y_ref.1), kind=kLoop, calls=%fused_computation.31 | loop fusion | bytes 7077888 | tf_op jit(solution)/shard_map/slice | solution.py:371
  13.0 1.3 collective-permute-start.1
  14.2 5.8 %collective-permute-start = (f32[54,2,32,128]{3,2,1,0:T(8,128)}, f32[54,2,32,128]{3,2,1,0:T(8,128)}, u32[]{:S(2)}, u32[]{:S(2)}) collective-permute-start(f32[54,2,32,128]{3,2,1,0:T(8,128)} %get-tuple-element.82), channel_id=1, source_target_pairs={{0,4},{4,8},{8,12},{12,16},{16,20},{20,24},{24,28},{28,32},{32,36}... | collective-permute-start | bytes 5308424 | tf_op jit(solution)/shard_map/ppermute | solution.py:370
  20.1 0.7 slice.264
  20.8 0.7 slice_bitcast_fusion.4
  21.5 0.8 slice.263
  22.3 2.4 %fusion.4 = (f32[54,4,2,128]{3,2,1,0:T(2,128)}, f32[54,4,2,128]{3,2,1,0:T(2,128)}) fusion(f32[54,4,32,128]{3,2,1,0:T(8,128)} %y_ref.1), kind=kLoop, calls=%fused_computation.30 | loop fusion | bytes 884736 | tf_op jit(solution)/shard_map/slice | solution.py:373
  25.4 0.9 slice_convert_fusion
  26.6 51.5 %all_gather.3.pk_ref = f32[9,16384]{1,0:T(8,128)} all-gather(f32[9,4096]{1,0:T(8,128)S(1)} %concatenate.28), channel_id=1, replica_groups=mesh['space'=64,'group'=4] {'group'}, dimensions={1}, use_global_device_ids=true | all-gather | bytes 737280 | tf_op jit(solution)/shard_map/all_gather | solution.py:351
  78.2 0.6 copy-done.11
  78.8 2.1 %collective-permute-start.6 = (f32[6,6,1,128]{3,2,1,0:T(1,128)S(1)}, f32[6,6,1,128]{3,2,1,0:T(1,128)S(1)}, u32[]{:S(2)}, u32[]{:S(2)}) collective-permute-start(f32[6,6,1,128]{3,2,1,0:T(1,128)S(1)} %pad_maximum_fusion.2), channel_id=1, source_target_pairs={{1,0},{2,1},{3,2},{5,4},{6,5},{7,6},{9,8},{10,9},{11,10},{13,12},{... | collective-permute-start | bytes 55304 | tf_op jit(solution)/shard_map/ppermute | solution.py:368
  81.0 4.4 %collective-permute-done.6.yrow_ref = f32[6,6,1,128]{3,2,1,0:T(1,128)S(1)} collective-permute-done((f32[6,6,1,128]{3,2,1,0:T(1,128)S(1)}, f32[6,6,1,128]{3,2,1,0:T(1,128)S(1)}, u32[]{:S(2)}, u32[]{:S(2)}) %collective-permute-start.6) | collective-permute-done | bytes 18464 | tf_op jit(solution)/shard_map/ppermute | solution.py:368
  85.4 0.6 copy-done.13
  86.0 1.2 copy-done.1
  87.2 0.9 copy-done.3
  88.2 0.8 copy-done.6
  89.0 0.8 copy-done.8
  89.8 0.9 copy-done.10
  90.7 0.9 copy-done.12
  91.6 0.7 copy-done.14
  92.4 21.0 %parcels.1 = (f32[7,4,32,128]{3,2,1,0:T(8,128)}, f32[7,1,32,128]{3,2,1,0:T(8,128)S(1)}, f32[7,1,32,128]{3,2,1,0:T(8,128)S(1)}, f32[7,6,1,128]{3,2,1,0:T(1,128)S(...) custom-call(s32[2]{0:T(128)S(1)} %pad_add_fusion.info_ref, f32[9,16384]{1,0:T(8,128)S(1)} %copy-done.1, ...), custom_call_target="tpu_custom_call" | custom-call | tf_op jit(solution)/shard_map/parcels/pallas_call | solution.py:379
  113.4 2.1 %collective-permute-start.7 = (f32[7,6,1,128]{3,2,1,0:T(1,128)S(1)}, f32[7,6,1,128]{3,2,1,0:T(1,128)S(1)}, u32[]{:S(2)}, u32[]{:S(2)}) collective-permute-start(f32[7,6,1,128]{3,2,1,0:T(1,128)S(1)} %get-tuple-element.71), channel_id=1, source_target_pairs={{0,1},{1,2},{2,3},{4,5},{5,6},{6,7},{8,9},{9,10},{10,11},{12,13},{... | collective-permute-start | bytes 64520 | tf_op jit(solution)/shard_map/ppermute | solution.py:429
  115.5 3.9 %spread.1 = f32[8,16384]{1,0:T(8,128)S(1)} custom-call(s32[8,128]{1,0:T(8,128)S(1)} %get-tuple-element.74.off_ref, f32[128,128]{1,0:T(8,128)S(1)} %get-tuple-element.75.dst_ref, f32[8,16640]{1,0:T(8,128)S(1)} %get-tuple-element.76.state_ref), custom_call_target="tpu_custom_call" | custom-call | tf_op jit(solution)/shard_map/spread/pallas_call | solution.py:438
  119.3 0.8 copy-done.2
  120.1 0.7 constant_dynamic-slice_fusion.2
  121.5 2.9 %collective-permute-start.11 = (f32[8,4096]{1,0:T(8,128)}, f32[8,4096]{1,0:T(8,128)}, u32[]{:S(2)}, u32[]{:S(2)}) collective-permute-start(f32[8,4096]{1,0:T(8,128)} %get-tuple-element.85), channel_id=1, source_target_pairs={{0,2},{1,3},{2,0},{3,1},{4,6},{5,7},{6,4},{7,5},{8,10},{9,11},{10,... | collective-permute-start | bytes 393224 | tf_op jit(solution)/shard_map/ppermute | solution.py:455
  124.3 1.5 slice_add_fusion.5
  125.9 1.6 scatter-add.16
  127.4 0.8 slice_add_fusion.6
  128.2 1.4 scatter-add.21
  129.6 1.4 scatter-add.19
  131.0 2.8 %collective-permute-start.3 = (f32[54,4,2,128]{3,2,1,0:T(2,128)}, f32[54,4,2,128]{3,2,1,0:T(2,128)S(1)}, u32[]{:S(2)}, u32[]{:S(2)}) collective-permute-start(f32[54,4,2,128]{3,2,1,0:T(2,128)} %get-tuple-element.79), channel_id=1, source_target_pairs={{1,0},{2,1},{3,2},{5,4},{6,5},{7,6},{9,8},{10,9},{11,10},{13,12},{... | collective-permute-start | bytes 663560 | tf_op jit(solution)/shard_map/ppermute | solution.py:373
  133.8 4.5 %collective-permute-start.2 = (f32[54,4,2,128]{3,2,1,0:T(2,128)}, f32[54,4,2,128]{3,2,1,0:T(2,128)S(1)}, u32[]{:S(2)}, u32[]{:S(2)}) collective-permute-start(f32[54,4,2,128]{3,2,1,0:T(2,128)} %get-tuple-element.80), channel_id=1, source_target_pairs={{0,1},{1,2},{2,3},{4,5},{5,6},{6,7},{8,9},{9,10},{10,11},{12,13},{... | collective-permute-start | bytes 663560 | tf_op jit(solution)/shard_map/ppermute | solution.py:372
  138.3 1.3 collective-permute-start.8
  139.6 1.9 %fusion = f32[5,4096]{1,0:T(8,128)} fusion(f32[8,4096]{1,0:T(8,128)} %collective-permute-done.12, f32[8,4096]{1,0:T(8,128)} %collective-permute-done.11, f32[8,4096]{1,0:T(8,128)} %collective-permute-done.10, f32[8,16384]{1,0:T(8,128)} %copy-done.2, s32[]{:T(128)S(6)} %select_n.31, f32[3,4096]{1,0:T(4,128)} %param.28, f32[1,4096]{1,0:T(1,128)} %bitcast.23, ...), kind=kLoop, calls=%fused_computation.1 | loop fusion | flops 122880 | bytes 495620 | tf_op jit(solution)/shard_map/jit(_where)/select_n | solution.py:459
  141.7 1.3 collective-permute-start.9
  143.0 1.6 fusion.2
  144.5 3.4 %collective-permute-done.9 = f32[7,1,32,128]{3,2,1,0:T(8,128)S(1)} collective-permute-done((f32[7,1,32,128]{3,2,1,0:T(8,128)}, f32[7,1,32,128]{3,2,1,0:T(8,128)S(1)}, u32[]{:S(2)}, u32[]{:S(2)}) %collective-permute-start.9) | collective-permute-done | bytes 114720 | tf_op jit(solution)/shard_map/ppermute | solution.py:433
  148.0 1.6 fusion.1.vap_ref
  149.6 0.9 copy-done.4
  150.5 1.0 copy-done.5
  151.5 0.8 copy-done.7
  152.3 9.4 %transport.1 = f32[54,4,32,128]{3,2,1,0:T(8,128)} custom-call(f32[54]{0:T(128)S(1)} %copy-done.15, f32[54,4,32,128]{3,2,1,0:T(8,128)S(1)} %copy-done, f32[54,2,32,128]{3,2,1,0:T(8,128)} %collective-permute-done.xlo_ref, f32[54,2,32,128]{3,2,1,0:T(8,128)} %collective-permute-done.1.xhi_ref, f32[54,4,2,128]{3,2,1,0:T(2,128)S(1)} %collective-permute-done.2.ylo_ref, ...), custom_call_target="tpu_custom_call" | custom-call | tf_op jit(solution)/shard_map/transport/pallas_call | solution.py:464
  (55 shorter events, 1.3 us)
Async XLA Ops:
  3.0 75.1 %collective-permute-start.4 = (f32[6,1,32,128]{3,2,1,0:T(8,128)S(1)}, f32[6,1,32,128]{3,2,1,0:T(8,128)S(1)}, u32[]{:S(2)}, u32[]{:S(2)}) collective-permute-start(f32[6,1,32,128]{3,2,1,0:T(8,128)S(1)} %pad_maximum_fusion), channel_id=1, source_target_pairs={{0,4},{4,8},{8,12},{12,16},{16,20},{20,24},{24,28},{28,32},{32,36}... | collective-permute-start | bytes 294920 | tf_op jit(solution)/shard_map/ppermute | solution.py:360
  7.0 19.4 %copy-start.19 = (f32[8,4096]{1,0:T(8,128)S(1)}, f32[8,4096]{1,0:T(8,128)}, u32[]{:S(2)}) copy-start(f32[8,4096]{1,0:T(8,128)} %param.30) | copy-start | bytes 393220
  7.0 19.5 %copy-start.18 = (f32[3,4096]{1,0:T(4,128)S(1)}, f32[3,4096]{1,0:T(4,128)}, u32[]{:S(2)}) copy-start(f32[3,4096]{1,0:T(4,128)} %param.28) | copy-start | bytes 147460
  7.0 19.5 %copy-start.20 = (f32[4096]{0:T(1024)S(1)}, f32[4096]{0:T(1024)}, u32[]{:S(2)}) copy-start(f32[4096]{0:T(1024)} %param.26) | copy-start | bytes 49156
  7.0 19.5 %copy-start.21 = (f32[4096]{0:T(1024)S(1)}, f32[4096]{0:T(1024)}, u32[]{:S(2)}) copy-start(f32[4096]{0:T(1024)} %param.27) | copy-start | bytes 49156
  7.0 71.1 %collective-permute-start.5 = (f32[6,1,32,128]{3,2,1,0:T(8,128)S(1)}, f32[6,1,32,128]{3,2,1,0:T(8,128)S(1)}, u32[]{:S(2)}, u32[]{:S(2)}) collective-permute-start(f32[6,1,32,128]{3,2,1,0:T(8,128)S(1)} %pad_maximum_fusion.1), channel_id=1, source_target_pairs={{4,0},{8,4},{12,8},{16,12},{20,16},{24,20},{28,24},{32,28},{36,32}... | collective-permute-start | bytes 294920 | tf_op jit(solution)/shard_map/ppermute | solution.py:361
  13.0 136.6 %collective-permute-start.1 = (f32[54,2,32,128]{3,2,1,0:T(8,128)}, f32[54,2,32,128]{3,2,1,0:T(8,128)}, u32[]{:S(2)}, u32[]{:S(2)}) collective-permute-start(f32[54,2,32,128]{3,2,1,0:T(8,128)} %get-tuple-element.81), channel_id=1, source_target_pairs={{4,0},{8,4},{12,8},{16,12},{20,16},{24,20},{28,24},{32,28},{36,32}... | collective-permute-start | bytes 5308424 | tf_op jit(solution)/shard_map/ppermute | solution.py:371
  14.2 135.3 %collective-permute-start = (f32[54,2,32,128]{3,2,1,0:T(8,128)}, f32[54,2,32,128]{3,2,1,0:T(8,128)}, u32[]{:S(2)}, u32[]{:S(2)}) collective-permute-start(f32[54,2,32,128]{3,2,1,0:T(8,128)} %get-tuple-element.82), channel_id=1, source_target_pairs={{0,4},{4,8},{8,12},{12,16},{16,20},{20,24},{24,28},{28,32},{32,36}... | collective-permute-start | bytes 5308424 | tf_op jit(solution)/shard_map/ppermute | solution.py:370
  78.1 2.9 %copy-start.9 = (f32[6,1,32,128]{3,2,1,0:T(8,128)}, f32[6,1,32,128]{3,2,1,0:T(8,128)S(1)}, u32[]{:S(2)}) copy-start(f32[6,1,32,128]{3,2,1,0:T(8,128)S(1)} %collective-permute-done.4.lo_ref) | copy-start | bytes 294916
  78.2 0.6 copy-start.11
  78.8 6.6 %collective-permute-start.6 = (f32[6,6,1,128]{3,2,1,0:T(1,128)S(1)}, f32[6,6,1,128]{3,2,1,0:T(1,128)S(1)}, u32[]{:S(2)}, u32[]{:S(2)}) collective-permute-start(f32[6,6,1,128]{3,2,1,0:T(1,128)S(1)} %pad_maximum_fusion.2), channel_id=1, source_target_pairs={{1,0},{2,1},{3,2},{5,4},{6,5},{7,6},{9,8},{10,9},{11,10},{13,12},{... | collective-permute-start | bytes 55304 | tf_op jit(solution)/shard_map/ppermute | solution.py:368
  85.4 0.6 copy-start.13
  86.0 1.2 copy-start.1
  87.2 0.9 copy-start.3
  88.2 0.8 copy-start.6
  89.0 0.8 copy-start.8
  89.8 0.9 copy-start.10
  90.7 0.9 copy-start.12
  91.6 0.7 copy-start.14
  92.4 57.2 %copy-start = (f32[54,4,32,128]{3,2,1,0:T(8,128)S(1)}, f32[54,4,32,128]{3,2,1,0:T(8,128)}, u32[]{:S(2)}) copy-start(f32[54,4,32,128]{3,2,1,0:T(8,128)} %y_ref.1) | copy-start | bytes 10616836
  113.4 7.5 %copy-start.16 = (f32[7,1,32,128]{3,2,1,0:T(8,128)}, f32[7,1,32,128]{3,2,1,0:T(8,128)S(1)}, u32[]{:S(2)}) copy-start(f32[7,1,32,128]{3,2,1,0:T(8,128)S(1)} %get-tuple-element.72) | copy-start | bytes 344068
  113.4 7.5 %copy-start.17 = (f32[7,1,32,128]{3,2,1,0:T(8,128)}, f32[7,1,32,128]{3,2,1,0:T(8,128)S(1)}, u32[]{:S(2)}) copy-start(f32[7,1,32,128]{3,2,1,0:T(8,128)S(1)} %get-tuple-element.73) | copy-start | bytes 344068
  113.4 36.2 %copy-start.15 = (f32[54]{0:T(128)S(1)}, f32[54]{0:T(128)}, u32[]{:S(2)}) copy-start(f32[54]{0:T(128)} %diff_ref.1) | copy-start | bytes 652
  113.4 8.1 %collective-permute-start.7 = (f32[7,6,1,128]{3,2,1,0:T(1,128)S(1)}, f32[7,6,1,128]{3,2,1,0:T(1,128)S(1)}, u32[]{:S(2)}, u32[]{:S(2)}) collective-permute-start(f32[7,6,1,128]{3,2,1,0:T(1,128)S(1)} %get-tuple-element.71), channel_id=1, source_target_pairs={{0,1},{1,2},{2,3},{4,5},{5,6},{6,7},{8,9},{9,10},{10,11},{12,13},{... | collective-permute-start | bytes 64520 | tf_op jit(solution)/shard_map/ppermute | solution.py:429
  119.3 0.8 copy-start.2
  120.9 10.1 %collective-permute-start.10 = (f32[8,4096]{1,0:T(8,128)}, f32[8,4096]{1,0:T(8,128)}, u32[]{:S(2)}, u32[]{:S(2)}) collective-permute-start(f32[8,4096]{1,0:T(8,128)} %get-tuple-element.83), channel_id=1, source_target_pairs={{0,1},{1,2},{2,3},{3,0},{4,5},{5,6},{6,7},{7,4},{8,9},{9,10},{10,1... | collective-permute-start | bytes 393224 | tf_op jit(solution)/shard_map/ppermute | solution.py:455
  120.9 12.9 %collective-permute-start.12 = (f32[8,4096]{1,0:T(8,128)}, f32[8,4096]{1,0:T(8,128)}, u32[]{:S(2)}, u32[]{:S(2)}) collective-permute-start(f32[8,4096]{1,0:T(8,128)} %get-tuple-element.84), channel_id=1, source_target_pairs={{0,3},{1,0},{2,1},{3,2},{4,7},{5,4},{6,5},{7,6},{8,11},{9,8},{10,9... | collective-permute-start | bytes 393224 | tf_op jit(solution)/shard_map/ppermute | solution.py:455
  121.5 2.9 %copy-start.22 = (f32[7,6,1,128]{3,2,1,0:T(1,128)}, f32[7,6,1,128]{3,2,1,0:T(1,128)S(1)}, u32[]{:S(2)}) copy-start(f32[7,6,1,128]{3,2,1,0:T(1,128)S(1)} %collective-permute-done.7) | copy-start | bytes 64516
  121.5 16.8 %collective-permute-start.11 = (f32[8,4096]{1,0:T(8,128)}, f32[8,4096]{1,0:T(8,128)}, u32[]{:S(2)}, u32[]{:S(2)}) collective-permute-start(f32[8,4096]{1,0:T(8,128)} %get-tuple-element.85), channel_id=1, source_target_pairs={{0,2},{1,3},{2,0},{3,1},{4,6},{5,7},{6,4},{7,5},{8,10},{9,11},{10,... | collective-permute-start | bytes 393224 | tf_op jit(solution)/shard_map/ppermute | solution.py:455
  131.0 18.5 %collective-permute-start.3 = (f32[54,4,2,128]{3,2,1,0:T(2,128)}, f32[54,4,2,128]{3,2,1,0:T(2,128)S(1)}, u32[]{:S(2)}, u32[]{:S(2)}) collective-permute-start(f32[54,4,2,128]{3,2,1,0:T(2,128)} %get-tuple-element.79), channel_id=1, source_target_pairs={{1,0},{2,1},{3,2},{5,4},{6,5},{7,6},{9,8},{10,9},{11,10},{13,12},{... | collective-permute-start | bytes 663560 | tf_op jit(solution)/shard_map/ppermute | solution.py:373
  133.8 15.7 %collective-permute-start.2 = (f32[54,4,2,128]{3,2,1,0:T(2,128)}, f32[54,4,2,128]{3,2,1,0:T(2,128)S(1)}, u32[]{:S(2)}, u32[]{:S(2)}) collective-permute-start(f32[54,4,2,128]{3,2,1,0:T(2,128)} %get-tuple-element.80), channel_id=1, source_target_pairs={{0,1},{1,2},{2,3},{4,5},{5,6},{6,7},{8,9},{9,10},{10,11},{12,13},{... | collective-permute-start | bytes 663560 | tf_op jit(solution)/shard_map/ppermute | solution.py:372
  138.3 3.4 %collective-permute-start.8 = (f32[7,1,32,128]{3,2,1,0:T(8,128)}, f32[7,1,32,128]{3,2,1,0:T(8,128)S(1)}, u32[]{:S(2)}, u32[]{:S(2)}) collective-permute-start(f32[7,1,32,128]{3,2,1,0:T(8,128)} %scatter-add.19), channel_id=1, source_target_pairs={{0,4},{4,8},{8,12},{12,16},{16,20},{20,24},{24,28},{28,32},{32,36}... | collective-permute-start | bytes 344072 | tf_op jit(solution)/shard_map/ppermute | solution.py:432
  141.7 6.3 %collective-permute-start.9 = (f32[7,1,32,128]{3,2,1,0:T(8,128)}, f32[7,1,32,128]{3,2,1,0:T(8,128)S(1)}, u32[]{:S(2)}, u32[]{:S(2)}) collective-permute-start(f32[7,1,32,128]{3,2,1,0:T(8,128)} %scatter-add.21), channel_id=1, source_target_pairs={{4,0},{8,4},{12,8},{16,12},{20,16},{24,20},{28,24},{32,28},{36,32}... | collective-permute-start | bytes 344072 | tf_op jit(solution)/shard_map/ppermute | solution.py:433
  149.6 0.9 copy-start.4
  150.5 1.0 copy-start.5
  151.5 0.8 copy-start.7

commit v2 on v1

--- a/solution.py
+++ b/solution.py
@@ -1,3 +1,5 @@
+import functools
+
 import jax
 import jax.numpy as jnp
 from jax import lax
@@ -14,6 +16,8 @@
 courant = 0.3
 
 LANES = 128
+PARTS = (54,)
+MANY = 6
 CHUNK = 512
 PHYS = 1024
 WINDOW = 256
@@ -78,14 +82,15 @@
     vel_ref,
     fuel_ref,
     hi_ref,
-    yrow_ref,
+    ynext_ref,
+    ylast_ref,
     main_ref,
     dlo_ref,
     dhi_ref,
-    dy_ref,
     state_ref,
+    own_dst_ref,
+    off_ref,
     dst_ref,
-    off_ref,
     cell_scr,
     off_smem,
     sem,
@@ -107,7 +112,8 @@
         cell_scr[b : b + 1, :] = pk_ref[8:9, b * LANES : (b + 1) * LANES]
     cell = cell_scr[...].astype(jnp.int32)
     slot = iota((blocks, LANES), 0) * LANES + iota((blocks, LANES), 1)
-    mine = jnp.logical_and(slot < count, ((cell >> 12) & 3) == group)
+    y_of = ((cell >> 7) & 127) - group * 32
+    mine = jnp.logical_and(slot < count, jnp.logical_and(y_of >= -1, y_of < 32))
     ones = jnp.where(mine, 1.0, 0.0).astype(BF16)
     before = jnp.where(iota((LANES, LANES), 0) < iota((LANES, LANES), 1), 1.0, 0.0).astype(BF16)
     after = jnp.where(iota((LANES, LANES), 1) < iota((LANES, LANES), 0), 1.0, 0.0).astype(BF16)
@@ -115,7 +121,9 @@
     within = jnp.dot(ones, before, preferred_element_type=F32)
     row_sum = jnp.dot(ones, full, preferred_element_type=F32).astype(BF16)
     offset = jnp.dot(after, row_sum, preferred_element_type=F32)
-    dst_ref[...] = jnp.where(mine, within + offset, -1.0)
+    dst = jnp.where(mine, within + offset, -1.0)
+    dst_ref[...] = dst
+    own_dst_ref[...] = jnp.where(y_of >= 0, dst, -1.0)
     counts = lax.dot_general(jnp.ones((16, LANES), BF16), ones, NT, preferred_element_type=F32)
     counts = counts.astype(BF16)
     starts = jnp.dot(counts, before, preferred_element_type=F32)
@@ -130,7 +138,7 @@
         cells = jnp.broadcast_to(pk_ref[8:9, at], (8, 2048)).astype(jnp.int32)
         row = iota((8, 2048), 0)
         place = jnp.where(
-            row == 0, cells >> 14, jnp.where(row == 1, (cells >> 7) & 31, cells & 127)
+            row == 0, cells >> 14, jnp.where(row == 1, ((cells >> 7) & 127) - group * 32, cells & 127)
         ).astype(F32)
         high, low = halves(jnp.concatenate([pk_ref[0:8, at], place], axis=0))
         pieces[0:16, at] = high
@@ -153,7 +161,8 @@
             else:
                 block = own[f][x - 1]
             row_scr[x * YPAD : x * YPAD + rows, :] = block
-            row_scr[x * YPAD + rows : x * YPAD + rows + 1, :] = yrow_ref[f, x]
+            row_scr[x * YPAD + rows : x * YPAD + rows + 1, :] = ynext_ref[f, x]
+            row_scr[(x + 1) * YPAD - 1 : (x + 1) * YPAD, :] = ylast_ref[f, x]
         high, low = halves(row_scr[...].T)
         at = slice(f * LANES, (f + 1) * LANES)
         ft[at, 0:256] = high
@@ -187,7 +196,8 @@
         fx, fy, fz = cv[0:1, at], cv[1:2, at], cv[2:3, at]
         x0, z0 = cv[8:9, at], cv[10:11, at]
         y0 = jnp.where(valid, cv[9:10, at], 1000.0)
-        wy = hat(iota((YPAD, CHUNK), 0).astype(F32), y0, fy)
+        line = iota((YPAD, CHUNK), 0)
+        wy = hat(jnp.where(line == YPAD - 1, -1, line).astype(F32), y0, fy)
         parts = [wy * hat(float(x), x0, fx) for x in range(planes + 2)]
         parts.append(jnp.zeros((256 - (planes + 2) * YPAD, CHUNK), F32))
         high, low = halves(jnp.concatenate(parts, axis=0))
@@ -241,36 +251,118 @@
                 dhi_ref[k, 0] = block
             else:
                 main_ref[k, x - 1] = block
-            dy_ref[k, x] = cells[x * YPAD + rows : x * YPAD + rows + 1]
-
-
-def spread_kernel(off_ref, dst_ref, state_ref, out_ref, both_scr):
+
+
+def spread_kernel(info_ref, off_ref, dst_ref, state_ref, *outs_and_scratch):
+    outs, both_scr = outs_and_scratch[:-1], outs_and_scratch[-1]
     high, low = halves(state_ref[...])
     both_scr[0:16, :] = jnp.concatenate([high, low], axis=0)
-
-    def spread(i, carry):
-        for j in range(8):
-            b = i * 8 + j
-            aligned = (off_ref[0, b] >> 7) << 7
-            hot = one_hot(dst_ref[pl.ds(b, 1), :], aligned)
-            block = both_scr[:, pl.ds(pl.multiple_of(aligned, LANES), WINDOW)]
-            got = jnp.dot(block, hot, preferred_element_type=F32)
-            out_ref[:, pl.ds(pl.multiple_of(b * LANES, LANES), LANES)] = got[0:8] + got[8:16]
-        return carry
-
-    lax.fori_loop(0, dst_ref.shape[0] // 8, spread, 0)
-
-
-def species_kernel(
-    diff_ref, y_ref, xlo_ref, xhi_ref, ylo_ref, yhi_ref, ux_ref, dens_ref, vap_ref, out_ref, pad
+    group = info_ref[1]
+    each = dst_ref.shape[0] // len(outs)
+    for d, out in enumerate(outs):
+        owner = lax.rem(group + d, len(outs))
+
+        def spread(i, carry):
+            for j in range(8):
+                b = owner * each + i * 8 + j
+                aligned = (off_ref[0, b] >> 7) << 7
+                hot = one_hot(dst_ref[pl.ds(b, 1), :], aligned)
+                block = both_scr[:, pl.ds(pl.multiple_of(aligned, LANES), WINDOW)]
+                got = jnp.dot(block, hot, preferred_element_type=F32)
+                at = pl.ds(pl.multiple_of((i * 8 + j) * LANES, LANES), LANES)
+                out[:, at] = got[0:8] + got[8:16]
+            return carry
+
+        lax.fori_loop(0, each // 8, spread, 0)
+
+
+def prepare_kernel(
+    cells_ref,
+    weights_ref,
+    radius_ref,
+    temp_ref,
+    velocity_ref,
+    gas_temp_ref,
+    dens_ref,
+    vel_ref,
+    fuel_ref,
+    species_ref,
+    packed_ref,
+    top_ref,
+    bottom_ref,
+    *outs_and_sems,
 ):
+    outs, sems = outs_and_sems[:-1], outs_and_sems[-1]
+    planes = gas_temp_ref.shape[0]
+    rows = gas_temp_ref.shape[1]
+    copies = []
+
+    def take(source, target):
+        copies.append(pltpu.make_async_copy(source, target, sems.at[len(copies)]))
+        copies[-1].start()
+
+    at = 0
+    for c, size in enumerate(PARTS):
+        take(species_ref.at[at : at + size, planes - 2 : planes], outs[2 * c])
+        take(species_ref.at[at : at + size, 0:2], outs[2 * c + 1])
+        at += size
+    take(species_ref.at[:, :, rows - 2 : rows], outs[2 * len(PARTS)])
+    take(species_ref.at[:, :, 0:2], outs[2 * len(PARTS) + 1])
+    w = [weights_ref[c : c + 1, :] for c in range(8)]
+    packed_ref[0:1, :] = (w[4] + w[5]) + (w[6] + w[7])
+    packed_ref[1:2, :] = (w[2] + w[3]) + (w[6] + w[7])
+    packed_ref[2:3, :] = (w[1] + w[3]) + (w[5] + w[7])
+    packed_ref[3:4, :] = radius_ref[...].reshape(1, -1)
+    packed_ref[4:5, :] = temp_ref[...].reshape(1, -1)
+    packed_ref[5:8, :] = velocity_ref[...]
+    packed_ref[8:9, :] = cells_ref[0:1, :].astype(F32)
+    own = [gas_temp_ref, dens_ref, vel_ref.at[0], vel_ref.at[1], vel_ref.at[2], fuel_ref.at[0]]
+    for f in range(6):
+        top_ref[f, 0] = own[f][planes - 1]
+        bottom_ref[f, 0] = own[f][0]
+    for copy in copies:
+        copy.wait()
+
+
+def transport_kernel(
+    first_part,
+    first_block,
+    edge_ref,
+    diff_ref,
+    y_ref,
+    xlo_ref,
+    xhi_ref,
+    ylo_ref,
+    yhi_ref,
+    ux_ref,
+    dens_ref,
+    *rest,
+):
+    if first_part:
+        main_ref, below_ref, above_ref, out_ref, gas_ref, pad = rest
+
+        @pl.when(pl.program_id(0) == 0)
+        def _():
+            last = main_ref.shape[1] - 1
+            for k in range(main_ref.shape[0]):
+                for x in range(last + 1):
+                    total = main_ref[k, x]
+                    if x == 0:
+                        total = total + below_ref[k, 0]
+                    if x == last:
+                        total = total + above_ref[k, 0]
+                    gas_ref[k, x] = total
+
+        vap_ref = gas_ref.at[0]
+    else:
+        vap_ref, _, out_ref, pad = rest
     species, planes, rows, depth = y_ref.shape
     at = iota((rows, depth), 1)
     left1 = jnp.where(at >= 1, 16.0, 0.0)
     left2 = jnp.where(at >= 2, -1.0, 0.0)
     right1 = jnp.where(at < depth - 1, 16.0, 0.0)
     right2 = jnp.where(at < depth - 2, -1.0, 0.0)
-    first = pl.program_id(0) * species
+    first = (first_block + pl.program_id(0)) * species
     for x in range(planes):
         speed = ux_ref[x] * (courant / 12.0)
         gain = source_coef * vap_ref[x] / dens_ref[x]
@@ -280,16 +372,16 @@
 
             def plane(i):
                 if i < 0:
-                    return xlo_ref[s, i + 2]
+                    return xlo_ref[s, i + 2] * edge_ref[0]
                 if i >= planes:
-                    return xhi_ref[s, i - planes]
+                    return xhi_ref[s, i - planes] * edge_ref[1]
                 return y_ref[s, i]
 
             center = plane(x)
             up1, up2, dn1, dn2 = plane(x + 1), plane(x + 2), plane(x - 1), plane(x - 2)
-            pad[6:8, :] = ylo_ref[s, x]
+            pad[6:8, :] = ylo_ref[s, x] * edge_ref[2]
             pad[8 : 8 + rows, :] = center
-            pad[8 + rows : 10 + rows, :] = yhi_ref[s, x]
+            pad[8 + rows : 10 + rows, :] = yhi_ref[s, x] * edge_ref[3]
             near = up1 + dn1 + pad[7 : 7 + rows, :] + pad[9 : 9 + rows, :]
             far = up2 + dn2 + pad[6 : 6 + rows, :] + pad[10 : 10 + rows, :]
             along = (
@@ -327,56 +419,69 @@
     capacity = drop_radius.shape[0]
     slots = capacity * groups
     blocks = slots // LANES
-    ahead = [(i, i + 1) for i in range(count_s - 1)]
+    ahead = [(i, (i + 1) % count_s) for i in range(count_s)]
     back = [(b, a) for a, b in ahead]
-    g_ahead = [(i, i + 1) for i in range(groups - 1)]
+    g_ahead = [(i, (i + 1) % groups) for i in range(groups)]
     g_back = [(b, a) for a, b in g_ahead]
-    group = lax.axis_index("group")
-
-    def upper(chosen):
-        return sum(parcel_weights[c : c + 1] for c in chosen)
-
-    packed = jnp.concatenate(
-        [
-            upper((4, 5, 6, 7)),
-            upper((2, 3, 6, 7)),
-            upper((1, 3, 5, 7)),
-            drop_radius[None],
-            drop_temp[None],
-            drop_velocity,
-            parcel_cells[0:1].astype(F32),
-        ],
-        axis=0,
-    )
-    parcels = lax.all_gather(packed, "group", axis=1, tiled=True)
-
-    def rim(x):
-        return jnp.concatenate(
-            [gas_temp[None, x : x + 1], gas_density[None, x : x + 1], gas_velocity[:, x : x + 1],
-             species[0:1, x : x + 1]],
-            axis=0,
-        )
-
-    field_lo = lax.ppermute(rim(planes - 1), "space", ahead)
-    field_hi = lax.ppermute(rim(0), "space", back)
-    own_row = jnp.concatenate(
-        [gas_temp[None, :, 0:1], gas_density[None, :, 0:1], gas_velocity[:, :, 0:1],
-         species[0:1, :, 0:1]],
-        axis=0,
-    )
-    row = jnp.concatenate([field_lo[:, :, 0:1], own_row, field_hi[:, :, 0:1]], axis=1)
-    row = lax.ppermute(row, "group", g_back)
-
-    x_lo = lax.ppermute(species[:, planes - 2 :], "space", ahead)
-    x_hi = lax.ppermute(species[:, 0:2], "space", back)
-    y_lo = lax.ppermute(species[:, :, rows - 2 :], "group", g_ahead)
-    y_hi = lax.ppermute(species[:, :, 0:2], "group", g_back)
-
+    space, group = lax.axis_index("space"), lax.axis_index("group")
     info = jnp.stack([parcel_counts[0], group.astype(jnp.int32)])
+    edge = jnp.stack([space > 0, space < count_s - 1, group > 0, group < groups - 1]).astype(F32)
+
     whole = lambda shape: pl.BlockSpec(shape, lambda i, n=len(shape): (0,) * n)
     smem = pl.BlockSpec(memory_space=pltpu.SMEM)
+    hbm = pl.BlockSpec(memory_space=pl.ANY)
+    shaped = lambda *shape: jax.ShapeDtypeStruct(shape, F32)
+    limit = pltpu.CompilerParams(vmem_limit_bytes=62 * 2**20)
+
+    sizes = [size for size in PARTS for _ in range(2)]
+    prepared = pl.pallas_call(
+        prepare_kernel,
+        grid=(1,),
+        in_specs=[
+            whole((8, capacity)),
+            whole((8, capacity)),
+            whole((capacity,)),
+            whole((capacity,)),
+            whole((3, capacity)),
+            whole((planes, rows, depth)),
+            whole((planes, rows, depth)),
+            whole((3, planes, rows, depth)),
+            whole((1, planes, rows, depth)),
+            hbm,
+        ],
+        out_specs=[whole((9, capacity)), whole((6, 1, rows, depth)), whole((6, 1, rows, depth))]
+        + [hbm] * (len(sizes) + 2),
+        out_shape=[shaped(9, capacity), shaped(6, 1, rows, depth), shaped(6, 1, rows, depth)]
+        + [shaped(size, 2, rows, depth) for size in sizes]
+        + [shaped(kinds, planes, 2, depth)] * 2,
+        scratch_shapes=[pltpu.SemaphoreType.DMA((len(sizes) + 2,))],
+        compiler_params=limit,
+        name="prepare",
+    )(
+        parcel_cells, parcel_weights, drop_radius, drop_temp, drop_velocity,
+        gas_temp, gas_density, gas_velocity, species, species,
+    )
+    packed, top, bottom = prepared[0:3]
+    parcels = lax.all_gather(packed, "group", axis=1, tiled=True)
+    field_lo = lax.ppermute(top, "space", ahead)
+    field_hi = lax.ppermute(bottom, "space", back)
+
+    def line(y):
+        at = slice(y, y + 1)
+        own = [gas_temp[None, :, at], gas_density[None, :, at], gas_velocity[:, :, at],
+               species[0:1, :, at]]
+        own = jnp.concatenate(own, axis=0)
+        return jnp.concatenate([field_lo[:, :, at], own, field_hi[:, :, at]], axis=1)
+
+    y_next = lax.ppermute(line(0), "group", g_back)
+    y_last = lax.ppermute(line(rows - 1), "group", g_ahead)
+    x_lo = [lax.ppermute(prepared[3 + 2 * c], "space", ahead) for c in range(len(PARTS))]
+    x_hi = [lax.ppermute(prepared[4 + 2 * c], "space", back) for c in range(len(PARTS))]
+    y_lo = lax.ppermute(prepared[-2], "group", g_ahead)
+    y_hi = lax.ppermute(prepared[-1], "group", g_back)
+
     reach = slots + WINDOW
-    main, dep_lo, dep_hi, dep_y, state, dst, off = pl.pallas_call(
+    main, dep_lo, dep_hi, state, dst, off = pl.pallas_call(
         parcel_kernel,
         grid=(1,),
         in_specs=[
@@ -389,26 +494,26 @@
             whole((1, planes, rows, depth)),
             whole((6, 1, rows, depth)),
             whole((6, planes + 2, 1, depth)),
+            whole((6, planes + 2, 1, depth)),
         ],
         out_specs=[
             whole((7, planes, rows, depth)),
             whole((7, 1, rows, depth)),
             whole((7, 1, rows, depth)),
-            whole((7, planes + 2, 1, depth)),
             whole((8, reach)),
             whole((blocks, LANES)),
             whole((8, LANES)),
         ],
         out_shape=[
-            jax.ShapeDtypeStruct((7, planes, rows, depth), F32),
-            jax.ShapeDtypeStruct((7, 1, rows, depth), F32),
-            jax.ShapeDtypeStruct((7, 1, rows, depth), F32),
-            jax.ShapeDtypeStruct((7, planes + 2, 1, depth), F32),
-            jax.ShapeDtypeStruct((8, reach), F32),
-            jax.ShapeDtypeStruct((blocks, LANES), F32),
+            shaped(7, planes, rows, depth),
+            shaped(7, 1, rows, depth),
+            shaped(7, 1, rows, depth),
+            shaped(8, reach),
+            shaped(blocks, LANES),
             jax.ShapeDtypeStruct((8, LANES), jnp.int32),
         ],
         scratch_shapes=[
+            pltpu.VMEM((blocks, LANES), F32),
             pltpu.VMEM((blocks, LANES), F32),
             pltpu.SMEM((8, LANES), jnp.int32),
             pltpu.SemaphoreType.DMA,
@@ -422,65 +527,77 @@
             pltpu.VMEM((8, slots), F32),
             pltpu.VMEM((7 * LANES, 256), F32),
         ],
-        compiler_params=pltpu.CompilerParams(vmem_limit_bytes=50 * 2**20),
+        compiler_params=limit,
         name="parcels",
-    )(info, parcels, field_lo, gas_temp, gas_density, gas_velocity, species, field_hi, row)
-
-    from_y = lax.ppermute(dep_y, "group", g_ahead)
-    dep_lo = dep_lo.at[:, :, 0:1].add(from_y[:, 0:1])
-    dep_hi = dep_hi.at[:, :, 0:1].add(from_y[:, planes + 1 :])
+    )(info, parcels, field_lo, gas_temp, gas_density, gas_velocity, species, field_hi, y_next, y_last)
+
     from_below = lax.ppermute(dep_hi, "space", ahead)
     from_above = lax.ppermute(dep_lo, "space", back)
-    gas_sources = main.at[:, :, 0:1].add(from_y[:, 1 : planes + 1])
-    gas_sources = gas_sources.at[:, 0:1].add(from_below)
-    gas_sources = gas_sources.at[:, planes - 1 :].add(from_above)
 
     spread = pl.pallas_call(
         spread_kernel,
         grid=(1,),
-        in_specs=[smem, whole((blocks, LANES)), whole((8, reach))],
-        out_specs=whole((8, slots)),
-        out_shape=jax.ShapeDtypeStruct((8, slots), F32),
+        in_specs=[smem, smem, whole((blocks, LANES)), whole((8, reach))],
+        out_specs=[whole((8, capacity))] * groups,
+        out_shape=[shaped(8, capacity)] * groups,
         scratch_shapes=[pltpu.VMEM((16, reach), BF16)],
-        compiler_params=pltpu.CompilerParams(vmem_limit_bytes=24 * 2**20),
+        compiler_params=limit,
         name="spread",
-    )(off, dst, state)
-
-    def part(owner):
-        return lax.dynamic_slice_in_dim(spread, owner * capacity, capacity, axis=1)
-
-    new_state = part(group)
+    )(info, off, dst, state)
+    new_state = spread[0]
     for d in range(1, groups):
         route = [(i, (i + d) % groups) for i in range(groups)]
-        new_state = new_state + lax.ppermute(part((group + d) % groups), "group", route)
+        new_state = new_state + lax.ppermute(spread[d], "group", route)
     old_state = jnp.concatenate([drop_radius[None], drop_temp[None], drop_velocity], axis=0)
     slot = group * capacity + jnp.arange(capacity, dtype=jnp.int32)
     live = slot < parcel_counts[0]
     parcel_state = jnp.where(live[None], new_state[0:5], old_state)
 
-    many = 6
-    by_kind = lambda *shape: pl.BlockSpec((many,) + shape, lambda i: (i, 0, 0, 0))
+    def by_kind(first, *shape):
+        return pl.BlockSpec((MANY,) + shape, lambda i: (first + i, 0, 0, 0))
+
     gas = pl.BlockSpec((planes, rows, depth), lambda i: (0, 0, 0))
-    species_next = pl.pallas_call(
-        species_kernel,
-        grid=(kinds // many,),
-        in_specs=[
-            smem,
-            by_kind(planes, rows, depth),
-            by_kind(2, rows, depth),
-            by_kind(2, rows, depth),
-            by_kind(planes, 2, depth),
-            by_kind(planes, 2, depth),
-            pl.BlockSpec((None, planes, rows, depth), lambda i: (0, 0, 0, 0)),
-            gas,
-            pl.BlockSpec((None, planes, rows, depth), lambda i: (0, 0, 0, 0)),
-        ],
-        out_specs=by_kind(planes, rows, depth),
-        out_shape=jax.ShapeDtypeStruct(species.shape, F32),
-        scratch_shapes=[pltpu.VMEM((rows + 16, depth), F32)],
-        compiler_params=pltpu.CompilerParams(vmem_limit_bytes=24 * 2**20),
-        name="transport",
-    )(diffusion, species, x_lo, x_hi, y_lo, y_hi, gas_velocity, gas_density, gas_sources)
+    row0 = pl.BlockSpec((None, planes, rows, depth), lambda i: (0, 0, 0, 0))
+    all_gas = whole((7, planes, rows, depth))
+    rim = whole((7, 1, rows, depth))
+    species_next = gas_sources = None
+    at = 0
+    for c, size in enumerate(PARTS):
+        first = at // MANY
+        at += size
+        out_specs = [by_kind(first, planes, rows, depth)]
+        out_shape = [shaped(*species.shape)]
+        if c == 0:
+            extra, extra_specs = (main, from_below, from_above), [all_gas, rim, rim]
+            out_specs.append(all_gas)
+            out_shape.append(shaped(7, planes, rows, depth))
+        else:
+            extra, extra_specs = (gas_sources, species_next), [row0, hbm]
+        got = pl.pallas_call(
+            functools.partial(transport_kernel, c == 0, first),
+            grid=(size // MANY,),
+            in_specs=[
+                smem,
+                smem,
+                by_kind(first, planes, rows, depth),
+                by_kind(0, 2, rows, depth),
+                by_kind(0, 2, rows, depth),
+                by_kind(first, planes, 2, depth),
+                by_kind(first, planes, 2, depth),
+                row0,
+                gas,
+            ]
+            + extra_specs,
+            out_specs=out_specs,
+            out_shape=out_shape,
+            input_output_aliases={} if c == 0 else {10: 0},
+            scratch_shapes=[pltpu.VMEM((rows + 16, depth), F32)],
+            compiler_params=limit,
+            name="transport",
+        )(edge, diffusion, species, x_lo[c], x_hi[c], y_lo, y_hi, gas_velocity, gas_density, *extra)
+        species_next = got[0]
+        if c == 0:
+            gas_sources = got[1]
     return (species_next, gas_sources, parcel_state)
 
 

time: 163 us -> 253 us (1.55)
  Pallas kernels: 34.3 us -> 155 us
  local copies, waits for them, and re-layouts: 28 us -> 3.68 us
  starting transfers between devices: 29.9 us -> 40.1 us
  blocking collectives: 51.5 us -> 43.8 us
  other arithmetic: 8.42 us -> 2.94 us
    pallas_call x2 -> x3, Pallas kernels: 13.3 us -> 139 us  [the longest x1 124 us: per_device(): pl.pallas_call(prepare_kernel, grid=(1,), in_specs=[whole((8, capacity)),...]
    ppermute x1, starting transfers between devices: 1.28 us -> 13.2 us  [per_device(): from_above = lax.ppermute(dep_lo, 'space', back)]
    unnamed x46 -> x14, local copies, waits for them, and re-layouts: 11.2 us -> 1.32 us
    slice x8 -> x4, local copies, waits for them, and re-layouts: 10 us -> 1.59 us  [the longest x1 0.83 us: line(): gas_velocity[:, :, at]]
    all_gather x1, blocking collectives: 51.5 us -> 43.8 us  [per_device(): parcels = lax.all_gather(packed, 'group', axis=1, tiled=True)]
    pallas_call x1, Pallas kernels: 21 us -> 15.9 us  [per_device(): pl.pallas_call(parcel_kernel, grid=(1,), in_specs=[smem, whole((9, slots)...]
    scatter-add x3 -> x0, local copies, waits for them, and re-layouts: 4.34 us -> none  [the longest x1 1.58 us: per_device(): gas_sources = main.at[:, :, 0:1].add(from_y[:, 1:planes + 1])]
    scatter-add x2 -> x0, other arithmetic: 3.13 us -> none  [the longest x1 1.57 us: per_device(): gas_sources = gas_sources.at[:, 0:1].add(from_below)]
  transfers between devices with their start and end apart: 13 -> 13, of which waited for: 3 -> 6; matrix products, arithmetic and copies ran while one was open for 14% -> 2% of each run, Pallas kernels for 15% -> 8%
where the time goes in v2:
time: 253 us; the launch traced here: 254 us
  Pallas kernels  155 us (61%)
  blocking collectives  43.8 us (17%)
  starting transfers between devices  40.1 us (16%)
  waiting for transfers between devices  6.99 us (3%)
  local copies, waits for them, and re-layouts  3.68 us (1%)
  other arithmetic  2.94 us (1%)
    pallas_call x1, Pallas kernels, per_device(): pl.pallas_call(prepare_kernel, grid=(1,), in_specs=[whole((8, capacity)),...  124 us
    all_gather x1, blocking collectives, per_device(): parcels = lax.all_gather(packed, 'group', axis=1, tiled=True)  43.8 us
    pallas_call x1, Pallas kernels, per_device(): pl.pallas_call(parcel_kernel, grid=(1,), in_specs=[smem, whole((9, slots)...  15.9 us
    ppermute x1, starting transfers between devices, per_device(): from_above = lax.ppermute(dep_lo, 'space', back)  13.2 us
    pallas_call x1, Pallas kernels, per_device(): pl.pallas_call(functools.partial(transport_kernel, c == 0, first), grid=(...  10.5 us
    ppermute x1, starting transfers between devices, per_device(): field_hi = lax.ppermute(bottom, 'space', back)  7.66 us
    ppermute x1, starting transfers between devices, per_device(): lax.ppermute(prepared[4 + 2 * c], 'space', back)  5.68 us
  transfers between devices with their start and end apart: 13, of which 6 were waited for; matrix products, arithmetic and copies ran while one was open for 2% of the time, Pallas kernels for 8%

profile of v2, /device:TPU:1, one launch (start us, length us, event | category | flops | bytes accessed | tf_op | source)
XLA Modules:
  0.0 254.1 jit_solution(6273720200400600400)
XLA Ops:
  0.6 123.7 %prepare.1 = (f32[9,4096]{1,0:T(8,128)}, f32[6,1,32,128]{3,2,1,0:T(8,128)}, f32[6,1,32,128]{3,2,1,0:T(8,128)}, f32[54,2,32,128]{3,2,1,0:T(8,128)}, f32[54,2,32,1...) custom-call(s32[8,4096]{1,0:T(8,128)} %cells_ref.1, f32[8,4096]{1,0:T(8,128)} %weights_ref.1, ...), custom_call_target="tpu_custom_call" | custom-call | tf_op jit(solution)/shard_map/prepare/pallas_call | solution.py:437
  124.3 2.1 collective-permute-start.4
  126.5 7.7 %collective-permute-start.5 = (f32[6,1,32,128]{3,2,1,0:T(8,128)}, f32[6,1,32,128]{3,2,1,0:T(8,128)S(1)}, u32[]{:S(2)}, u32[]{:S(2)}) collective-permute-start(f32[6,1,32,128]{3,2,1,0:T(8,128)} %get-tuple-element.28), channel_id=1, source_target_pairs={{4,0},{8,4},{12,8},{16,12},{20,16},{24,20},{28,24},{32,28},{36,32}... | collective-permute-start | bytes 294920 | tf_op jit(solution)/shard_map/ppermute | solution.py:467
  134.1 3.5 %collective-permute-start.2 = (f32[54,4,2,128]{3,2,1,0:T(2,128)}, f32[54,4,2,128]{3,2,1,0:T(2,128)}, u32[]{:S(2)}, u32[]{:S(2)}) collective-permute-start(f32[54,4,2,128]{3,2,1,0:T(2,128)} %get-tuple-element.24), channel_id=1, source_target_pairs={{0,1},{1,2},{2,3},{3,0},{4,5},{5,6},{6,7},{7,4},{8,9},{9,10},{10,1... | collective-permute-start | bytes 663560 | tf_op jit(solution)/shard_map/ppermute | solution.py:480
  137.6 0.0 collective-permute-start
  137.6 5.7 %collective-permute-start.1 = (f32[54,2,32,128]{3,2,1,0:T(8,128)}, f32[54,2,32,128]{3,2,1,0:T(8,128)}, u32[]{:S(2)}, u32[]{:S(2)}) collective-permute-start(f32[54,2,32,128]{3,2,1,0:T(8,128)} %get-tuple-element.23), channel_id=1, source_target_pairs={{4,0},{8,4},{12,8},{16,12},{20,16},{24,20},{28,24},{32,28},{36,32}... | collective-permute-start | bytes 5308424 | tf_op jit(solution)/shard_map/ppermute | solution.py:479
  143.3 0.7 fusion.1
  144.0 0.8 slice_bitcast_fusion
  144.8 0.8 fusion.2
  145.6 43.8 %all_gather.3.pk_ref = f32[9,16384]{1,0:T(8,128)} all-gather(f32[9,4096]{1,0:T(8,128)} %get-tuple-element.26), channel_id=1, replica_groups=mesh['space'=64,'group'=4] {'group'}, dimensions={1}, use_global_device_ids=true | all-gather | bytes 737280 | tf_op jit(solution)/shard_map/all_gather | solution.py:465
  190.0 0.0 collective-permute-done.4.lo_ref
  190.0 0.0 copy-start.5
  190.1 0.0 collective-permute-done.5.hi_ref
  190.1 0.0 copy-start.6
  190.1 0.2 collective-permute-start.6
  190.4 3.2 %collective-permute-start.7 = (f32[6,6,1,128]{3,2,1,0:T(1,128)S(1)}, f32[6,6,1,128]{3,2,1,0:T(1,128)}, u32[]{:S(2)}, u32[]{:S(2)}) collective-permute-start(f32[6,6,1,128]{3,2,1,0:T(1,128)S(1)} %pad_maximum_fusion.1), channel_id=1, source_target_pairs={{0,1},{1,2},{2,3},{3,0},{4,5},{5,6},{6,7},{7,4},{8,9},{9,10},{10,1... | collective-permute-start | bytes 55304 | tf_op jit(solution)/shard_map/ppermute | solution.py:477
  193.6 0.6 pad_add_fusion.info_ref
  194.1 0.0 copy-start.1
  194.1 1.1 collective-permute-done.6.ynext_ref
  195.2 0.0 collective-permute-done.7.ylast_ref
  195.2 0.0 copy-done.5
  195.2 0.0 copy-done.6
  195.3 15.9 %parcels.1 = (f32[7,4,32,128]{3,2,1,0:T(8,128)}, f32[7,1,32,128]{3,2,1,0:T(8,128)}, f32[7,1,32,128]{3,2,1,0:T(8,128)}, f32[8,16640]{1,0:T(8,128)}, f32[128,128]{1,0:T(8,128)}, /*index=5*/s32[8,128]{1,0:T(8,128)}) custom-call(s32[2]{0:T(128)} %pad_add_fusion.info_ref, f32[9,16384]{1,0:T(8,128)} %all_gather.3.pk_ref, f32[6,1,32,128]{3,2,1,0:T(8,128)} %copy-done.5, ...), custom_call_target="tpu_custom_call" | custom-call | tf_op jit(solution)/shard_map/parcels/pallas_call | solution.py:484
  211.2 5.0 %spread.1 = (f32[8,4096]{1,0:T(8,128)}, f32[8,4096]{1,0:T(8,128)}, f32[8,4096]{1,0:T(8,128)}, f32[8,4096]{1,0:T(8,128)}) custom-call(s32[2]{0:T(128)} %pad_add_fusion.info_ref, s32[8,128]{1,0:T(8,128)} %get-tuple-element.34.off_ref, f32[128,128]{1,0:T(8,128)} %get-tuple-element.35.dst_ref, f32[8,16640]{1,0:T(8,128)} %get-tuple-element.36.state_ref), custom_call_target="tpu_custom_call" | custom-call | tf_op jit(solution)/shard_map/spread/pallas_call | solution.py:537
  216.2 3.1 %collective-permute-start.10 = (f32[8,4096]{1,0:T(8,128)}, f32[8,4096]{1,0:T(8,128)S(1)}, u32[]{:S(2)}, u32[]{:S(2)}) collective-permute-start(f32[8,4096]{1,0:T(8,128)} %get-tuple-element.38), channel_id=1, source_target_pairs={{0,1},{1,2},{2,3},{3,0},{4,5},{5,6},{6,7},{7,4},{8,9},{9,10},{10,1... | collective-permute-start | bytes 393224 | tf_op jit(solution)/shard_map/ppermute | solution.py:550
  219.3 0.2 collective-permute-start.11
  219.4 0.0 collective-permute-done.2.ylo_ref
  219.5 0.3 collective-permute-start.12
  219.7 0.7 add_convert_fusion.edge_ref
  220.4 2.0 collective-permute-done.10
  222.4 1.1 collective-permute-start.3
  223.4 2.1 collective-permute-done.11
  225.5 0.0 collective-permute-start.8
  225.5 0.7 collective-permute-done.12
  226.2 13.2 %collective-permute-start.9 = (f32[7,1,32,128]{3,2,1,0:T(8,128)}, f32[7,1,32,128]{3,2,1,0:T(8,128)S(1)}, u32[]{:S(2)}, u32[]{:S(2)}) collective-permute-start(f32[7,1,32,128]{3,2,1,0:T(8,128)} %get-tuple-element.31), channel_id=1, source_target_pairs={{4,0},{8,4},{12,8},{16,12},{20,16},{24,20},{28,24},{32,28},{36,32}... | collective-permute-start | bytes 344072 | tf_op jit(solution)/shard_map/ppermute | solution.py:535
  239.4 0.0 copy-done.1
  239.4 1.6 fusion
  241.1 0.0 collective-permute-done.3.yhi_ref
  241.1 0.0 copy-start.2
  241.1 0.6 collective-permute-done.8.rest_1_
  241.7 0.5 collective-permute-done.9.rest_2_
  242.2 0.0 collective-permute-done.xlo_ref
  242.2 0.0 copy-done.2
  242.2 0.0 collective-permute-done.1.xhi_ref
  242.2 0.6 copy-done.4
  242.9 0.0 copy-done.3
  242.9 0.7 copy-done
  243.5 10.5 %transport.1 = (f32[54,4,32,128]{3,2,1,0:T(8,128)}, f32[7,4,32,128]{3,2,1,0:T(8,128)}) custom-call(f32[4]{0:T(128)} %add_convert_fusion.edge_ref, f32[54]{0:T(128)} %diff_ref.1, f32[54,4,32,128]{3,2,1,0:T(8,128)} %y_ref.1, f32[54,2,32,128]{3,2,1,0:T(8,128)} %copy-done, f32[54,2,32,128]{3,2,1,0:T(8,128)} %collective-permute-done.1.xhi_ref, ...), custom_call_target="tpu_custom_call" | custom-call | tf_op jit(solution)/shard_map/transport/pallas_call | solution.py:576
  (8 shorter events, 0.1 us)
Async XLA Ops:
  124.3 65.7 %collective-permute-start.4 = (f32[6,1,32,128]{3,2,1,0:T(8,128)}, f32[6,1,32,128]{3,2,1,0:T(8,128)S(1)}, u32[]{:S(2)}, u32[]{:S(2)}) collective-permute-start(f32[6,1,32,128]{3,2,1,0:T(8,128)} %get-tuple-element.27), channel_id=1, source_target_pairs={{0,4},{4,8},{8,12},{12,16},{16,20},{20,24},{24,28},{28,32},{32,36}... | collective-permute-start | bytes 294920 | tf_op jit(solution)/shard_map/ppermute | solution.py:466
  126.5 63.6 %collective-permute-start.5 = (f32[6,1,32,128]{3,2,1,0:T(8,128)}, f32[6,1,32,128]{3,2,1,0:T(8,128)S(1)}, u32[]{:S(2)}, u32[]{:S(2)}) collective-permute-start(f32[6,1,32,128]{3,2,1,0:T(8,128)} %get-tuple-element.28), channel_id=1, source_target_pairs={{4,0},{8,4},{12,8},{16,12},{20,16},{24,20},{28,24},{32,28},{36,32}... | collective-permute-start | bytes 294920 | tf_op jit(solution)/shard_map/ppermute | solution.py:467
  134.1 85.3 %collective-permute-start.2 = (f32[54,4,2,128]{3,2,1,0:T(2,128)}, f32[54,4,2,128]{3,2,1,0:T(2,128)}, u32[]{:S(2)}, u32[]{:S(2)}) collective-permute-start(f32[54,4,2,128]{3,2,1,0:T(2,128)} %get-tuple-element.24), channel_id=1, source_target_pairs={{0,1},{1,2},{2,3},{3,0},{4,5},{5,6},{6,7},{7,4},{8,9},{9,10},{10,1... | collective-permute-start | bytes 663560 | tf_op jit(solution)/shard_map/ppermute | solution.py:480
  137.6 104.7 %collective-permute-start = (f32[54,2,32,128]{3,2,1,0:T(8,128)}, f32[54,2,32,128]{3,2,1,0:T(8,128)S(1)}, u32[]{:S(2)}, u32[]{:S(2)}) collective-permute-start(f32[54,2,32,128]{3,2,1,0:T(8,128)} %get-tuple-element.22), channel_id=1, source_target_pairs={{0,4},{4,8},{8,12},{12,16},{16,20},{20,24},{24,28},{28,32},{32,36}... | collective-permute-start | bytes 5308424 | tf_op jit(solution)/shard_map/ppermute | solution.py:478
  137.6 104.7 %collective-permute-start.1 = (f32[54,2,32,128]{3,2,1,0:T(8,128)}, f32[54,2,32,128]{3,2,1,0:T(8,128)}, u32[]{:S(2)}, u32[]{:S(2)}) collective-permute-start(f32[54,2,32,128]{3,2,1,0:T(8,128)} %get-tuple-element.23), channel_id=1, source_target_pairs={{4,0},{8,4},{12,8},{16,12},{20,16},{24,20},{28,24},{32,28},{36,32}... | collective-permute-start | bytes 5308424 | tf_op jit(solution)/shard_map/ppermute | solution.py:479
  190.0 5.2 %copy-start.5 = (f32[6,1,32,128]{3,2,1,0:T(8,128)}, f32[6,1,32,128]{3,2,1,0:T(8,128)S(1)}, u32[]{:S(2)}) copy-start(f32[6,1,32,128]{3,2,1,0:T(8,128)S(1)} %collective-permute-done.4.lo_ref) | copy-start | bytes 294916
  190.1 5.2 %copy-start.6 = (f32[6,1,32,128]{3,2,1,0:T(8,128)}, f32[6,1,32,128]{3,2,1,0:T(8,128)S(1)}, u32[]{:S(2)}) copy-start(f32[6,1,32,128]{3,2,1,0:T(8,128)S(1)} %collective-permute-done.5.hi_ref) | copy-start | bytes 294916
  190.1 5.1 %collective-permute-start.6 = (f32[6,6,1,128]{3,2,1,0:T(1,128)S(1)}, f32[6,6,1,128]{3,2,1,0:T(1,128)}, u32[]{:S(2)}, u32[]{:S(2)}) collective-permute-start(f32[6,6,1,128]{3,2,1,0:T(1,128)S(1)} %pad_maximum_fusion), channel_id=1, source_target_pairs={{1,0},{2,1},{3,2},{0,3},{5,4},{6,5},{7,6},{4,7},{9,8},{10,9},{11,1... | collective-permute-start | bytes 55304 | tf_op jit(solution)/shard_map/ppermute | solution.py:476
  190.4 4.9 %collective-permute-start.7 = (f32[6,6,1,128]{3,2,1,0:T(1,128)S(1)}, f32[6,6,1,128]{3,2,1,0:T(1,128)}, u32[]{:S(2)}, u32[]{:S(2)}) collective-permute-start(f32[6,6,1,128]{3,2,1,0:T(1,128)S(1)} %pad_maximum_fusion.1), channel_id=1, source_target_pairs={{0,1},{1,2},{2,3},{3,0},{4,5},{5,6},{6,7},{7,4},{8,9},{9,10},{10,1... | collective-permute-start | bytes 55304 | tf_op jit(solution)/shard_map/ppermute | solution.py:477
  194.1 45.3 %copy-start.1 = (f32[3,4096]{1,0:T(4,128)S(1)}, f32[3,4096]{1,0:T(4,128)}, u32[]{:S(2)}) copy-start(f32[3,4096]{1,0:T(4,128)} %velocity_ref.1) | copy-start | bytes 147460
  216.2 6.2 %collective-permute-start.10 = (f32[8,4096]{1,0:T(8,128)}, f32[8,4096]{1,0:T(8,128)S(1)}, u32[]{:S(2)}, u32[]{:S(2)}) collective-permute-start(f32[8,4096]{1,0:T(8,128)} %get-tuple-element.38), channel_id=1, source_target_pairs={{0,1},{1,2},{2,3},{3,0},{4,5},{5,6},{6,7},{7,4},{8,9},{9,10},{10,1... | collective-permute-start | bytes 393224 | tf_op jit(solution)/shard_map/ppermute | solution.py:550
  219.3 6.2 %collective-permute-start.11 = (f32[8,4096]{1,0:T(8,128)}, f32[8,4096]{1,0:T(8,128)S(1)}, u32[]{:S(2)}, u32[]{:S(2)}) collective-permute-start(f32[8,4096]{1,0:T(8,128)} %get-tuple-element.39), channel_id=1, source_target_pairs={{0,2},{1,3},{2,0},{3,1},{4,6},{5,7},{6,4},{7,5},{8,10},{9,11},{10,... | collective-permute-start | bytes 393224 | tf_op jit(solution)/shard_map/ppermute | solution.py:550
  219.5 6.8 %collective-permute-start.12 = (f32[8,4096]{1,0:T(8,128)}, f32[8,4096]{1,0:T(8,128)S(1)}, u32[]{:S(2)}, u32[]{:S(2)}) collective-permute-start(f32[8,4096]{1,0:T(8,128)} %get-tuple-element.40), channel_id=1, source_target_pairs={{0,3},{1,0},{2,1},{3,2},{4,7},{5,4},{6,5},{7,6},{8,11},{9,8},{10,9... | collective-permute-start | bytes 393224 | tf_op jit(solution)/shard_map/ppermute | solution.py:550
  222.4 18.7 %collective-permute-start.3 = (f32[54,4,2,128]{3,2,1,0:T(2,128)}, f32[54,4,2,128]{3,2,1,0:T(2,128)S(1)}, u32[]{:S(2)}, u32[]{:S(2)}) collective-permute-start(f32[54,4,2,128]{3,2,1,0:T(2,128)} %get-tuple-element.25), channel_id=1, source_target_pairs={{1,0},{2,1},{3,2},{0,3},{5,4},{6,5},{7,6},{4,7},{9,8},{10,9},{11,1... | collective-permute-start | bytes 663560 | tf_op jit(solution)/shard_map/ppermute | solution.py:481
  225.5 16.1 %collective-permute-start.8 = (f32[7,1,32,128]{3,2,1,0:T(8,128)}, f32[7,1,32,128]{3,2,1,0:T(8,128)S(1)}, u32[]{:S(2)}, u32[]{:S(2)}) collective-permute-start(f32[7,1,32,128]{3,2,1,0:T(8,128)} %get-tuple-element.30), channel_id=1, source_target_pairs={{0,4},{4,8},{8,12},{12,16},{16,20},{20,24},{24,28},{28,32},{32,36}... | collective-permute-start | bytes 344072 | tf_op jit(solution)/shard_map/ppermute | solution.py:534
  226.2 16.0 %collective-permute-start.9 = (f32[7,1,32,128]{3,2,1,0:T(8,128)}, f32[7,1,32,128]{3,2,1,0:T(8,128)S(1)}, u32[]{:S(2)}, u32[]{:S(2)}) collective-permute-start(f32[7,1,32,128]{3,2,1,0:T(8,128)} %get-tuple-element.31), channel_id=1, source_target_pairs={{4,0},{8,4},{12,8},{16,12},{20,16},{24,20},{28,24},{32,28},{36,32}... | collective-permute-start | bytes 344072 | tf_op jit(solution)/shard_map/ppermute | solution.py:535
  241.1 1.1 copy-start.2
  241.7 1.2 copy-start.3
  242.2 0.7 copy-start.4
  242.2 1.3 copy-start
